TPU v7x, 256 devices: a whole 4x4x8 slice. The times are simulated.
256 devices in a mesh: range: 16 (over z, core), az: 16 (over y, x).
Axes of the slice: x: 4, y: 4, z: 8, core: 2. Of those that a mesh axis runs over, the one named last changes fastest.
Arguments:
- return_integer_lag: int32 [16, 128, 8], P('az'), may hold values from 0 to 32703
- return_fractional_lag: float32 [16, 128, 8], P('az'), may hold values from 0 to 8
- return_field_strength: float32 [16, 128, 8], P('az'), may hold values from 0.1 to 0.6
- sector_emit_offset: int32 [16], P('az'), may hold values from 0 to 63
- sector_active_returns: int32 [16], P('az'), may hold values from 1 to 8, as said below
- ambient_photon_flux: float32 [128], replicated, may hold values from 0.2 to 1
- coded_emission_spectrum: float32 [128, 2, 16384], P('range', None, 'az'), may hold values from -6 to 6
Outputs:
- histogram: float32 [16, 128, 16384], P('az', None, 'range')
Inputs may be any that keep to these rules, and one draw needn't show every extreme that they name: `sector_active_returns`: slots below a column's count are live; some column has all 8 slots live and some column only one.
All inputs are finite; a program needn't handle non-finite values.
Results may differ from a plain program's by a relative error of at most 0.0003.
Values sent between devices are 32-bit elements; how exact they have to be, the bound alone decides.
A program may use at most 64 MiB of HBM per device.

v0:
```python
import functools
import math

import jax
import jax.numpy as jnp
from jax import lax
from jax.experimental import pallas as pl
from jax.experimental.pallas import tpu as pltpu
from jax.sharding import PartitionSpec as P

TIME_SLOTS = 16384
SIDE = 128
BEAMS = 8
SLOTS = 8
GROUP = 16
MESH = pl.DeviceIdType.MESH
F32 = jnp.float32
BF16 = jnp.bfloat16


def iota(shape, dim):
    return lax.broadcasted_iota(jnp.int32, shape, dim)


def cos_sin(turns):
    x = (turns - jnp.round(turns)) * math.pi
    y = x * x
    s = -1.0 / 39916800 * y + 1.0 / 362880
    s = s * y - 1.0 / 5040
    s = s * y + 1.0 / 120
    s = s * y - 1.0 / 6
    s = (s * y + 1.0) * x
    c = 1.0 / 479001600 * y - 1.0 / 3628800
    c = c * y + 1.0 / 40320
    c = c * y - 1.0 / 720
    c = c * y + 1.0 / 24
    c = c * y - 0.5
    c = c * y + 1.0
    return 1.0 - 2.0 * s * s, 2.0 * s * c


def split(x):
    hi = x.astype(BF16)
    return hi, (x - hi.astype(F32)).astype(BF16)


def dot(a, b):
    return jnp.dot(a, b, preferred_element_type=F32)


def dot3(a_hi, a_lo, b_hi, b_lo):
    return dot(a_hi, b_hi) + dot(a_hi, b_lo) + dot(a_lo, b_hi)


def blocks(a, b, c, d):
    return jnp.concatenate(
        [jnp.concatenate([a, b], axis=1), jnp.concatenate([c, d], axis=1)], axis=0
    )


def dft_tables():
    row, col = iota((SIDE, SIDE), 0), iota((SIDE, SIDE), 1)
    c, s = cos_sin(((row * col) & (SIDE - 1)).astype(F32) * (1.0 / SIDE))
    left = split(blocks(c, -s, s, c))
    right = split(blocks(c, s, -s, c))
    twist = cos_sin((row * col).astype(F32) * (1.0 / TIME_SLOTS))
    return left, right, twist


def prefix_tables():
    row, col = iota((SIDE, SIDE), 0), iota((SIDE, SIDE), 1)
    upper = jnp.where(row < col, 1.0, 0.0).astype(F32)
    ones = jnp.ones((SIDE, SIDE), F32)
    lower = jnp.where(col < row, 1.0, 0.0).astype(F32)
    inner = blocks(upper, ones, upper, ones).astype(BF16)
    outer = jnp.concatenate([lower, lower], axis=1).astype(BF16)
    return inner, outer


def as_column(near, far):
    near_rows = jnp.concatenate(
        [jnp.broadcast_to(near[b : b + 1], (2 * SLOTS, SLOTS)) for b in range(BEAMS)], axis=0
    )
    far_rows = jnp.concatenate(
        [jnp.broadcast_to(far[b : b + 1], (2 * SLOTS, SLOTS)) for b in range(BEAMS)], axis=0
    )
    row, col = iota((SIDE, SLOTS), 0), iota((SIDE, SLOTS), 1)
    rows = jnp.where((row & SLOTS) == 0, near_rows, far_rows)
    return jnp.sum(jnp.where((row & (SLOTS - 1)) == col, rows, 0.0), axis=1, keepdims=True)


def as_row(column):
    row, col = iota((SIDE, SIDE), 0), iota((SIDE, SIDE), 1)
    wide = jnp.broadcast_to(column, (SIDE, SIDE))
    return jnp.sum(jnp.where(row == col, wide, 0.0), axis=0, keepdims=True)


def phase_tables(near, far):
    delay, frac, amp = [as_column(n, f) for n, f in zip(near, far)]
    row, col = iota((SIDE, SIDE), 0), iota((SIDE, SIDE), 1)
    whole = (col * delay.astype(jnp.int32)) & (TIME_SLOTS - 1)
    inner_c, inner_s = cos_sin((whole.astype(F32) + col.astype(F32) * frac) * (1.0 / TIME_SLOTS))
    inner_c, inner_s = inner_c * amp, inner_s * amp
    near_row = (row & SLOTS) == 0
    parts = []
    for x in (inner_c, inner_s):
        parts.append(
            jnp.concatenate([jnp.where(near_row, x, 0.0), jnp.where(near_row, 0.0, x)], axis=1)
        )
    right = split(jnp.concatenate(parts, axis=0))
    signed = row - jnp.where(row >= SIDE // 2, SIDE, 0)
    whole = (signed * as_row(delay).astype(jnp.int32)) & (SIDE - 1)
    outer_c, outer_s = cos_sin((whole.astype(F32) + signed.astype(F32) * as_row(frac)) * (1.0 / SIDE))
    left = split(blocks(outer_c, -outer_s, -outer_s, -outer_c))
    return left, right


def spectrum(left, right, beam):
    mine = ((iota((2 * SIDE, 2 * SIDE), 0) & (SIDE - 1)) >> 4) == beam
    hi, lo = [jnp.where(mine, x.astype(F32), 0.0).astype(BF16) for x in right]
    return dot3(left[0], left[1], hi, lo)


def light_of(spec, pulse_real, pulse_imag, left, right, twist):
    spec_real, spec_imag = spec[:SIDE], spec[SIDE:]
    wide_real = jnp.concatenate([pulse_real, pulse_real], axis=1)
    wide_imag = jnp.concatenate([pulse_imag, pulse_imag], axis=1)
    filt = jnp.concatenate(
        [wide_real * spec_real - wide_imag * spec_imag, wide_real * spec_imag + wide_imag * spec_real],
        axis=0,
    )
    section = dot3(left[0], left[1], *split(filt))
    rows = []
    for trip in range(2):
        real = section[:SIDE, trip * SIDE : (trip + 1) * SIDE]
        imag = section[SIDE:, trip * SIDE : (trip + 1) * SIDE]
        rows.append(
            jnp.concatenate(
                [real * twist[0] - imag * twist[1], real * twist[1] + imag * twist[0]], axis=1
            )
        )
    hi, lo = split(jnp.concatenate(rows, axis=0))
    field = dot(hi, right[0]) + dot(hi, right[1]) + dot(lo, right[0])
    power = field * field
    power = power[:SIDE] + power[SIDE:]
    return power[:, :SIDE] + power[:, SIDE:]


def pile_up(power, ambient, inner, outer):
    flux = (power * (1.0 / TIME_SLOTS) + ambient) * (1.0 / TIME_SLOTS)
    flux = jnp.transpose(flux)
    hi, lo = split(flux)
    sums = dot(jnp.concatenate([hi, lo], axis=1), inner)
    within, totals = sums[:, :SIDE], sums[:, SIDE:]
    hi, lo = split(totals)
    before = within + dot(outer, jnp.concatenate([hi, lo], axis=0))
    series = 1.0 - flux * (1.0 / 6)
    for k in (5, 4, 3, 2):
        series = 1.0 - flux * (1.0 / k) * series
    detected = jnp.where(flux < 0.1, flux * series, 1.0 - jnp.exp(-flux))
    return TIME_SLOTS * detected * jnp.exp(-before)


def kernel(
    chunk,
    lag_ref, frac_ref, amp_ref, offset_ref, count_ref, ambient_ref, pulse_ref,
    out_ref,
    own, gathered, echo_out, echo_in, spec, left_tab, right_tab, twist_tab, inner_tab, outer_tab,
    ready, arrived,
    pulse_send, pulse_recv, echo_send, echo_recv, hist_send, hist_recv,
):
    me_range, me_az = lax.axis_index("range"), lax.axis_index("az")
    chunks = BEAMS // chunk
    barrier = pltpu.get_barrier_semaphore()

    def greet(k, carry):
        pl.semaphore_signal(barrier, inc=1, device_id={"az": lax.rem(me_az + k, GROUP)}, device_id_type=MESH)
        pl.semaphore_signal(barrier, inc=1, device_id={"range": lax.rem(me_range + k, GROUP)}, device_id_type=MESH)
        return carry

    lax.fori_loop(1, GROUP, greet, 0)

    for b in range(BEAMS):
        for part in range(2):
            for q in range(8):
                own[b, part, q : q + 1, :] = pulse_ref[b, part : part + 1, q * SIDE : (q + 1) * SIDE]
    first = pl.multiple_of(me_range * BEAMS, BEAMS)
    delay = lag_ref[0, pl.ds(first, BEAMS), :] + offset_ref[0]
    frac = frac_ref[0, pl.ds(first, BEAMS), :]
    amp = amp_ref[0, pl.ds(first, BEAMS), :]
    live = iota((BEAMS, SLOTS), 1) < count_ref[0]
    near_trip = delay < TIME_SLOTS
    near_amp = jnp.where(live & near_trip, amp, 0.0)
    far_amp = jnp.where(live & jnp.logical_not(near_trip), amp, 0.0)
    delay = delay.astype(F32)
    echo_out[...] = jnp.zeros_like(echo_out)
    echo_out[0, :, :SLOTS] = delay
    echo_out[1, :, :SLOTS] = frac
    echo_out[2, :, :SLOTS] = far_amp

    pl.semaphore_wait(barrier, 2 * (GROUP - 1))

    echo_copy = pltpu.make_async_remote_copy(
        src_ref=echo_out, dst_ref=echo_in, send_sem=echo_send, recv_sem=echo_recv,
        device_id={"az": lax.rem(me_az + 1, GROUP)}, device_id_type=MESH,
    )
    echo_copy.start()

    def send_pulses(i, carry):
        c = i // (GROUP - 1)
        k = lax.rem(i, GROUP - 1) + 1
        beams = pl.ds(c * chunk, chunk)
        pltpu.make_async_remote_copy(
            src_ref=own.at[beams], dst_ref=gathered.at[me_az, beams],
            send_sem=pulse_send, recv_sem=pulse_recv.at[c],
            device_id={"az": lax.rem(me_az + k, GROUP)}, device_id_type=MESH,
        ).start()
        return carry

    lax.fori_loop(0, chunks * (GROUP - 1), send_pulses, 0)
    gathered[me_az] = own[...]

    left, right, twist = dft_tables()
    for i in range(2):
        left_tab[i] = left[i]
        right_tab[i] = right[i]
        twist_tab[i] = twist[i]
    inner_tab[...], outer_tab[...] = prefix_tables()

    echo_copy.wait_recv()
    far = tuple(echo_in[i, :, :SLOTS] for i in range(3))
    echo_left, echo_right = phase_tables((delay, frac, near_amp), far)
    for b in range(BEAMS):
        spec[b] = spectrum(echo_left, echo_right, b)

    def work(c, carry):
        beams = pl.ds(c * chunk, chunk)
        some = gathered.at[pl.ds(0, GROUP - 1), beams]
        pltpu.make_async_remote_copy(
            src_ref=some, dst_ref=some, send_sem=pulse_send, recv_sem=pulse_recv.at[c],
            device_id={"az": me_az}, device_id_type=MESH,
        ).wait_recv()
        for j in range(chunk):
            b = c * chunk + j
            pulse_real = gathered[:, b, 0].reshape(SIDE, SIDE)
            pulse_imag = gathered[:, b, 1].reshape(SIDE, SIDE)
            power = light_of(
                spec[b], pulse_real, pulse_imag,
                (left_tab[0], left_tab[1]), (right_tab[0], right_tab[1]), (twist_tab[0], twist_tab[1]),
            )
            hist = pile_up(power, ambient_ref[first + b], inner_tab[...], outer_tab[...])
            for g in range(GROUP):
                ready[pl.ds(pl.multiple_of((g * BEAMS + b) * 8, 8), 8), :] = hist[g * 8 : (g + 1) * 8]
        here = pl.ds(pl.multiple_of((me_range * BEAMS + c * chunk) * 8, 8), chunk * 8)

        def send(k, carry):
            peer = lax.rem(me_range + k, GROUP)
            there = pl.ds(pl.multiple_of((peer * BEAMS + c * chunk) * 8, 8), chunk * 8)
            pltpu.make_async_remote_copy(
                src_ref=ready.at[there], dst_ref=arrived.at[here],
                send_sem=hist_send, recv_sem=hist_recv,
                device_id={"range": peer}, device_id_type=MESH,
            ).start()
            return carry

        lax.fori_loop(1, GROUP, send, 0)
        arrived[here, :] = ready[here, :]
        return carry

    lax.fori_loop(0, chunks, work, 0)

    most = pl.ds(0, (GROUP - 1) * BEAMS * 8)
    done = pltpu.make_async_remote_copy(
        src_ref=ready.at[most], dst_ref=arrived.at[most], send_sem=hist_send, recv_sem=hist_recv,
        device_id={"range": me_range}, device_id_type=MESH,
    )
    done.wait_recv()
    for g in range(GROUP):
        for s in range(8):
            out_ref[0, g * 8 : (g + 1) * 8, s * SIDE : (s + 1) * SIDE] = arrived[
                pl.ds(g * 64 + s, 8, stride=8), :
            ]
    done.wait_send()
    echo_copy.wait_send()
    pltpu.make_async_remote_copy(
        src_ref=gathered.at[pl.ds(0, GROUP - 1)], dst_ref=gathered.at[pl.ds(0, GROUP - 1)],
        send_sem=pulse_send, recv_sem=pulse_recv.at[0],
        device_id={"az": me_az}, device_id_type=MESH,
    ).wait_send()


def per_device(*arrays):
    chunk = 2
    vmem = pl.BlockSpec(memory_space=pltpu.VMEM)
    smem = pl.BlockSpec(memory_space=pltpu.SMEM)
    dma = pltpu.SemaphoreType.DMA
    return pl.pallas_call(
        functools.partial(kernel, chunk),
        out_shape=jax.ShapeDtypeStruct((1, GROUP * BEAMS, TIME_SLOTS // GROUP), F32),
        in_specs=[vmem, vmem, vmem, smem, smem, smem, vmem],
        out_specs=vmem,
        scratch_shapes=[
            pltpu.VMEM((BEAMS, 2, 8, SIDE), F32),
            pltpu.VMEM((GROUP, BEAMS, 2, 8, SIDE), F32),
            pltpu.VMEM((3, BEAMS, SIDE), F32),
            pltpu.VMEM((3, BEAMS, SIDE), F32),
            pltpu.VMEM((BEAMS, 2 * SIDE, 2 * SIDE), F32),
            pltpu.VMEM((2, 2 * SIDE, 2 * SIDE), BF16),
            pltpu.VMEM((2, 2 * SIDE, 2 * SIDE), BF16),
            pltpu.VMEM((2, SIDE, SIDE), F32),
            pltpu.VMEM((2 * SIDE, 2 * SIDE), BF16),
            pltpu.VMEM((SIDE, 2 * SIDE), BF16),
            pltpu.VMEM((GROUP * BEAMS * 8, SIDE), F32),
            pltpu.VMEM((GROUP * BEAMS * 8, SIDE), F32),
            dma, dma((BEAMS // chunk,)), dma, dma, dma, dma,
        ],
        compiler_params=pltpu.CompilerParams(
            collective_id=0, has_side_effects=True, vmem_limit_bytes=40 * 1024 * 1024
        ),
    )(*arrays)


def solution(mesh):
    in_specs = (
        P("az", None, None),
        P("az", None, None),
        P("az", None, None),
        P("az"),
        P("az"),
        P(),
        P("range", None, "az"),
    )
    out_specs = P("az", None, "range")
    return jax.shard_map(
        per_device, mesh=mesh, in_specs=in_specs, out_specs=out_specs, check_vma=False
    )
```

profile of v0, /device:TPU:1, one launch (start us, length us, event | category | flops | bytes accessed | tf_op | source)
XLA Modules:
  0.0 38.6 jit_solution(13002699458707539429)
XLA Ops:
  1.3 0.0 copy-start.2
  1.3 0.8 %copy.8.lag_ref = s32[1,128,8]{2,1,0:T(8,128)S(1)} copy(s32[1,128,8]{1,2,0:T(8,128)} %param.7) | data formatting | bytes 8192 | tf_op args[0]
  2.1 0.0 copy-done.2
  2.1 0.0 copy-start.3
  2.1 0.0 copy-start
  2.1 0.1 copy.9.frac_ref
  2.2 0.6 %copy-done.3 = f32[1,128,8]{1,2,0:T(8,128)S(1)} copy-done((f32[1,128,8]{1,2,0:T(8,128)S(1)}, f32[1,128,8]{1,2,0:T(8,128)}, u32[]{:S(2)}) %copy-start.3) | copy-done | bytes 4120
  2.8 0.0 copy-start.1
  2.8 0.1 copy.10.amp_ref
  2.9 0.1 copy-done
  3.0 0.5 %copy-done.1 = f32[128]{0:T(128)S(1)} copy-done((f32[128]{0:T(128)S(1)}, f32[128]{0:T(128)}, u32[]{:S(2)}) %copy-start.1) | copy-done | bytes 536
  3.5 34.3 %shard_map.73 = f32[1,128,1024]{2,1,0:T(8,128)S(1)} custom-call(s32[1,128,8]{2,1,0:T(8,128)S(1)} %copy.8.lag_ref, f32[1,128,8]{2,1,0:T(8,128)S(1)} %copy.9.frac_ref, f32[1,128,8]{2,1,0:T(8,128)S(1)} %copy.10.amp_ref, s32[1]{0:T(128)S(6)} %copy.12.offset_ref, s32[1]{0:T(128)S(6)} %copy.13.count_ref, f32[128]{0:T(128)S(1)} %copy-done.1, f32[8,2,1024]{2,1,0:T(2,128)S(1)} %copy-done), custom_call_target="tpu_custom_call" | custom-call | tf_op jit(solution)/shard_map/pallas_call | solution.py:297
  37.8 0.8 %copy.14 = f32[1,128,1024]{2,1,0:T(8,128)} copy(f32[1,128,1024]{2,1,0:T(8,128)S(1)} %shard_map.73) | data formatting | bytes 1048576
Async XLA Ops:
  1.3 0.8 %copy-start.2 = (f32[1,128,8]{1,2,0:T(8,128)S(1)}, f32[1,128,8]{1,2,0:T(8,128)}, u32[]{:S(2)}) copy-start(f32[1,128,8]{1,2,0:T(8,128)} %param.8) | copy-start | bytes 12292
  2.1 0.7 %copy-start.3 = (f32[1,128,8]{1,2,0:T(8,128)S(1)}, f32[1,128,8]{1,2,0:T(8,128)}, u32[]{:S(2)}) copy-start(f32[1,128,8]{1,2,0:T(8,128)} %param.9) | copy-start | bytes 12292
  2.1 0.8 %copy-start = (f32[8,2,1024]{2,1,0:T(2,128)S(1)}, f32[8,2,1024]{2,1,0:T(2,128)}, u32[]{:S(2)}) copy-start(f32[8,2,1024]{2,1,0:T(2,128)} %pulse_ref.1) | copy-start | bytes 196612
  2.8 0.7 %copy-start.1 = (f32[128]{0:T(128)S(1)}, f32[128]{0:T(128)}, u32[]{:S(2)}) copy-start(f32[128]{0:T(128)} %ambient_ref.1) | copy-start | bytes 1540
where the time goes:
time: 38.8 us; the launch traced here: 38.6 us
  Pallas kernels  34.3 us (88%)
  local copies, waits for them, and re-layouts  2.93 us (8%)
  between operations  1.34 us (3%)
    pallas_call x1, Pallas kernels, per_device(): pl.pallas_call(functools.partial(kernel, chunk), out_shape=jax.ShapeDtype...  34.3 us
    unnamed x12, local copies, waits for them, and re-layouts  2.93 us

commit v1 on v0

--- a/solution.py
+++ b/solution.py
@@ -1,4 +1,3 @@
-import functools
 import math
 
 import jax
@@ -13,6 +12,7 @@
 BEAMS = 8
 SLOTS = 8
 GROUP = 16
+SIDE_AZ = 4
 MESH = pl.DeviceIdType.MESH
 F32 = jnp.float32
 BF16 = jnp.bfloat16
@@ -78,15 +78,9 @@
 
 
 def as_column(near, far):
-    near_rows = jnp.concatenate(
-        [jnp.broadcast_to(near[b : b + 1], (2 * SLOTS, SLOTS)) for b in range(BEAMS)], axis=0
-    )
-    far_rows = jnp.concatenate(
-        [jnp.broadcast_to(far[b : b + 1], (2 * SLOTS, SLOTS)) for b in range(BEAMS)], axis=0
-    )
-    row, col = iota((SIDE, SLOTS), 0), iota((SIDE, SLOTS), 1)
-    rows = jnp.where((row & SLOTS) == 0, near_rows, far_rows)
-    return jnp.sum(jnp.where((row & (SLOTS - 1)) == col, rows, 0.0), axis=1, keepdims=True)
+    rows = jnp.concatenate([near, far] * BEAMS, axis=0)
+    row, col = iota((SIDE, SIDE), 0), iota((SIDE, SIDE), 1)
+    return jnp.sum(jnp.where((row >> 4) == col, rows, 0.0), axis=1, keepdims=True)
 
 
 def as_row(column):
@@ -162,63 +156,105 @@
 
 
 def kernel(
-    chunk,
+    lag_hbm, frac_hbm, amp_hbm, offset_hbm, count_hbm, ambient_hbm, pulse_hbm,
+    out_ref,
     lag_ref, frac_ref, amp_ref, offset_ref, count_ref, ambient_ref, pulse_ref,
-    out_ref,
-    own, gathered, echo_out, echo_in, spec, left_tab, right_tab, twist_tab, inner_tab, outer_tab,
+    gathered, echo_out, echo_in, spec, left_tab, right_tab, twist_tab, inner_tab, outer_tab,
     ready, arrived,
-    pulse_send, pulse_recv, echo_send, echo_recv, hist_send, hist_recv,
+    in_sem, first_send, first_recv, second_send, second_recv, echo_send, echo_recv,
+    hist_send, hist_recv, go_sem,
 ):
     me_range, me_az = lax.axis_index("range"), lax.axis_index("az")
-    chunks = BEAMS // chunk
+    y, x = me_az // SIDE_AZ, lax.rem(me_az, SIDE_AZ)
+    chief = GROUP - 1
+
+    def row_peer(k):
+        return y * SIDE_AZ + lax.rem(x + k, SIDE_AZ)
+
+    def column_peer(k):
+        return lax.rem(y + k, SIDE_AZ) * SIDE_AZ + x
+
+    def remote(src, dst, send, recv, **where):
+        return pltpu.make_async_remote_copy(
+            src_ref=src, dst_ref=dst, send_sem=send, recv_sem=recv, device_id=where, device_id_type=MESH
+        )
+
+    fetches = [
+        pltpu.make_async_copy(src, dst, in_sem.at[i])
+        for i, (src, dst) in enumerate(
+            (
+                (pulse_hbm, pulse_ref), (lag_hbm, lag_ref), (frac_hbm, frac_ref), (amp_hbm, amp_ref),
+                (offset_hbm, offset_ref), (count_hbm, count_ref), (ambient_hbm, ambient_ref),
+            )
+        )
+    ]
+    for fetch in fetches:
+        fetch.start()
+
     barrier = pltpu.get_barrier_semaphore()
-
-    def greet(k, carry):
-        pl.semaphore_signal(barrier, inc=1, device_id={"az": lax.rem(me_az + k, GROUP)}, device_id_type=MESH)
-        pl.semaphore_signal(barrier, inc=1, device_id={"range": lax.rem(me_range + k, GROUP)}, device_id_type=MESH)
-        return carry
-
-    lax.fori_loop(1, GROUP, greet, 0)
-
+    for k in range(1, SIDE_AZ):
+        for peer in (row_peer(k), column_peer(k)):
+            pl.semaphore_signal(barrier, inc=1, device_id={"az": peer}, device_id_type=MESH)
+    pl.semaphore_signal(
+        barrier, inc=1, device_id={"az": lax.rem(me_az + GROUP - 1, GROUP)}, device_id_type=MESH
+    )
+
+    @pl.when(me_range != chief)
+    def _():
+        pl.semaphore_signal(barrier, inc=1, device_id={"range": chief}, device_id_type=MESH)
+
+    fetches[0].wait()
     for b in range(BEAMS):
         for part in range(2):
             for q in range(8):
-                own[b, part, q : q + 1, :] = pulse_ref[b, part : part + 1, q * SIDE : (q + 1) * SIDE]
-    first = pl.multiple_of(me_range * BEAMS, BEAMS)
-    delay = lag_ref[0, pl.ds(first, BEAMS), :] + offset_ref[0]
-    frac = frac_ref[0, pl.ds(first, BEAMS), :]
-    amp = amp_ref[0, pl.ds(first, BEAMS), :]
-    live = iota((BEAMS, SLOTS), 1) < count_ref[0]
+                gathered[y, x, b, part, q : q + 1, :] = pulse_ref[
+                    b, part : part + 1, q * SIDE : (q + 1) * SIDE
+                ]
+    for fetch in fetches[1:]:
+        fetch.wait()
+    back = lax.rem(SIDE - me_range * BEAMS, SIDE)
+    delay = (lag_ref[0] + offset_ref[0]).astype(F32)
+    live = iota((SLOTS, SIDE), 0) < count_ref[0]
     near_trip = delay < TIME_SLOTS
+    amp = amp_ref[0]
     near_amp = jnp.where(live & near_trip, amp, 0.0)
     far_amp = jnp.where(live & jnp.logical_not(near_trip), amp, 0.0)
-    delay = delay.astype(F32)
-    echo_out[...] = jnp.zeros_like(echo_out)
-    echo_out[0, :, :SLOTS] = delay
-    echo_out[1, :, :SLOTS] = frac
-    echo_out[2, :, :SLOTS] = far_amp
-
-    pl.semaphore_wait(barrier, 2 * (GROUP - 1))
-
-    echo_copy = pltpu.make_async_remote_copy(
-        src_ref=echo_out, dst_ref=echo_in, send_sem=echo_send, recv_sem=echo_recv,
-        device_id={"az": lax.rem(me_az + 1, GROUP)}, device_id_type=MESH,
-    )
+    delay, frac, near_amp, far_amp = [
+        pltpu.roll(v, back, 1) for v in (delay, frac_ref[0], near_amp, far_amp)
+    ]
+    echo_out[0] = delay
+    echo_out[1] = frac
+    echo_out[2] = far_amp
+
+    @pl.when(me_range == chief)
+    def _():
+        pl.semaphore_wait(barrier, 2 * SIDE_AZ - 1 + GROUP - 1)
+
+    @pl.when(me_range != chief)
+    def _():
+        pl.semaphore_wait(barrier, 2 * SIDE_AZ - 1)
+
+    echo_copy = remote(echo_out, echo_in, echo_send, echo_recv, az=lax.rem(me_az + 1, GROUP))
     echo_copy.start()
 
-    def send_pulses(i, carry):
-        c = i // (GROUP - 1)
-        k = lax.rem(i, GROUP - 1) + 1
-        beams = pl.ds(c * chunk, chunk)
-        pltpu.make_async_remote_copy(
-            src_ref=own.at[beams], dst_ref=gathered.at[me_az, beams],
-            send_sem=pulse_send, recv_sem=pulse_recv.at[c],
-            device_id={"az": lax.rem(me_az + k, GROUP)}, device_id_type=MESH,
-        ).start()
+    def first_step(pair, carry):
+        b = 2 * pair
+        for k in (1, 3, 2):
+            mine = gathered.at[y, x, b]
+            remote(mine, mine, first_send, first_recv.at[b], az=row_peer(k)).start()
+            mine = gathered.at[y, x, b + 1]
+            remote(mine, mine, first_send, first_recv.at[b + 1], az=column_peer(k)).start()
         return carry
 
-    lax.fori_loop(0, chunks * (GROUP - 1), send_pulses, 0)
-    gathered[me_az] = own[...]
+    lax.fori_loop(0, BEAMS // 2, first_step, 0)
+
+    @pl.when(me_range == chief)
+    def _():
+        def tell(k, carry):
+            pl.semaphore_signal(go_sem, inc=1, device_id={"range": k}, device_id_type=MESH)
+            return carry
+
+        lax.fori_loop(0, GROUP - 1, tell, 0)
 
     left, right, twist = dft_tables()
     for i in range(2):
@@ -227,53 +263,76 @@
         twist_tab[i] = twist[i]
     inner_tab[...], outer_tab[...] = prefix_tables()
 
+    def second_step(pair, carry):
+        b = 2 * pair
+        for j in range(2):
+            three = gathered.at[0, pl.ds(0, SIDE_AZ - 1), b + j]
+            remote(three, three, first_send, first_recv.at[b + j], az=me_az).wait_recv()
+        for k in (1, 3, 2):
+            row = gathered.at[y, :, b]
+            remote(row, row, second_send, second_recv.at[b], az=column_peer(k)).start()
+            column = gathered.at[:, x, b + 1]
+            remote(column, column, second_send, second_recv.at[b + 1], az=row_peer(k)).start()
+        return carry
+
+    lax.fori_loop(0, BEAMS // 2, second_step, 0)
+
     echo_copy.wait_recv()
-    far = tuple(echo_in[i, :, :SLOTS] for i in range(3))
+    far = tuple(echo_in[i] for i in range(3))
     echo_left, echo_right = phase_tables((delay, frac, near_amp), far)
     for b in range(BEAMS):
         spec[b] = spectrum(echo_left, echo_right, b)
 
-    def work(c, carry):
-        beams = pl.ds(c * chunk, chunk)
-        some = gathered.at[pl.ds(0, GROUP - 1), beams]
-        pltpu.make_async_remote_copy(
-            src_ref=some, dst_ref=some, send_sem=pulse_send, recv_sem=pulse_recv.at[c],
-            device_id={"az": me_az}, device_id_type=MESH,
-        ).wait_recv()
-        for j in range(chunk):
-            b = c * chunk + j
-            pulse_real = gathered[:, b, 0].reshape(SIDE, SIDE)
-            pulse_imag = gathered[:, b, 1].reshape(SIDE, SIDE)
+    def send_tiles(peer, first_beam, count):
+        here = pl.ds(pl.multiple_of((me_range * BEAMS + first_beam) * 8, 8), count * 8)
+        there = pl.ds(pl.multiple_of((peer * BEAMS + first_beam) * 8, 8), count * 8)
+
+        @pl.when(peer != me_range)
+        def _():
+            remote(ready.at[there], arrived.at[here], hist_send, hist_recv, range=peer).start()
+
+    def work(pair, carry):
+        for j in range(2):
+            b = 2 * pair + j
+            twelve = gathered.at[pl.ds(0, SIDE_AZ - 1), :, b]
+            remote(twelve, twelve, second_send, second_recv.at[b], az=me_az).wait_recv()
+        for j in range(2):
+            b = 2 * pair + j
+            pulse_real = gathered[:, :, b, 0].reshape(SIDE, SIDE)
+            pulse_imag = gathered[:, :, b, 1].reshape(SIDE, SIDE)
             power = light_of(
                 spec[b], pulse_real, pulse_imag,
                 (left_tab[0], left_tab[1]), (right_tab[0], right_tab[1]), (twist_tab[0], twist_tab[1]),
             )
-            hist = pile_up(power, ambient_ref[first + b], inner_tab[...], outer_tab[...])
+            mine = iota((1, SIDE), 1) == me_range * BEAMS + b
+            ambient = jnp.sum(jnp.where(mine, ambient_ref[...], 0.0), axis=1, keepdims=True)
+            hist = pile_up(power, ambient, inner_tab[...], outer_tab[...])
             for g in range(GROUP):
                 ready[pl.ds(pl.multiple_of((g * BEAMS + b) * 8, 8), 8), :] = hist[g * 8 : (g + 1) * 8]
-        here = pl.ds(pl.multiple_of((me_range * BEAMS + c * chunk) * 8, 8), chunk * 8)
-
-        def send(k, carry):
-            peer = lax.rem(me_range + k, GROUP)
-            there = pl.ds(pl.multiple_of((peer * BEAMS + c * chunk) * 8, 8), chunk * 8)
-            pltpu.make_async_remote_copy(
-                src_ref=ready.at[there], dst_ref=arrived.at[here],
-                send_sem=hist_send, recv_sem=hist_recv,
-                device_id={"range": peer}, device_id_type=MESH,
-            ).start()
+
+        @pl.when((pair == 0) & (me_range != chief))
+        def _():
+            pl.semaphore_wait(go_sem, 1)
+
+        def send(peer, carry):
+            send_tiles(peer, 2 * pair, 2)
             return carry
 
-        lax.fori_loop(1, GROUP, send, 0)
-        arrived[here, :] = ready[here, :]
+        lax.fori_loop(0, GROUP // 2, send, 0)
         return carry
 
-    lax.fori_loop(0, chunks, work, 0)
+    lax.fori_loop(0, BEAMS // 2, work, 0)
+
+    def send_late(peer, carry):
+        send_tiles(peer, 0, BEAMS)
+        return carry
+
+    lax.fori_loop(GROUP // 2, GROUP, send_late, 0)
+    own = pl.ds(pl.multiple_of(me_range * BEAMS * 8, 8), BEAMS * 8)
+    arrived[own, :] = ready[own, :]
 
     most = pl.ds(0, (GROUP - 1) * BEAMS * 8)
-    done = pltpu.make_async_remote_copy(
-        src_ref=ready.at[most], dst_ref=arrived.at[most], send_sem=hist_send, recv_sem=hist_recv,
-        device_id={"range": me_range}, device_id_type=MESH,
-    )
+    done = remote(ready.at[most], arrived.at[most], hist_send, hist_recv, az=me_az)
     done.wait_recv()
     for g in range(GROUP):
         for s in range(8):
@@ -282,28 +341,32 @@
             ]
     done.wait_send()
     echo_copy.wait_send()
-    pltpu.make_async_remote_copy(
-        src_ref=gathered.at[pl.ds(0, GROUP - 1)], dst_ref=gathered.at[pl.ds(0, GROUP - 1)],
-        send_sem=pulse_send, recv_sem=pulse_recv.at[0],
-        device_id={"az": me_az}, device_id_type=MESH,
-    ).wait_send()
-
-
-def per_device(*arrays):
-    chunk = 2
-    vmem = pl.BlockSpec(memory_space=pltpu.VMEM)
-    smem = pl.BlockSpec(memory_space=pltpu.SMEM)
+    three = gathered.at[0, pl.ds(0, SIDE_AZ - 1)]
+    remote(three, three, first_send, first_recv.at[0], az=me_az).wait_send()
+    twelve = gathered.at[pl.ds(0, SIDE_AZ - 1)]
+    remote(twelve, twelve, second_send, second_recv.at[0], az=me_az).wait_send()
+
+
+def per_device(lag, frac, amp, offset, count, ambient, pulse):
+    lag, frac, amp = [jnp.swapaxes(v, 1, 2) for v in (lag, frac, amp)]
+    hbm = pl.BlockSpec(memory_space=pltpu.HBM)
     dma = pltpu.SemaphoreType.DMA
     return pl.pallas_call(
-        functools.partial(kernel, chunk),
+        kernel,
         out_shape=jax.ShapeDtypeStruct((1, GROUP * BEAMS, TIME_SLOTS // GROUP), F32),
-        in_specs=[vmem, vmem, vmem, smem, smem, smem, vmem],
-        out_specs=vmem,
+        in_specs=[hbm] * 7,
+        out_specs=pl.BlockSpec(memory_space=pltpu.VMEM),
         scratch_shapes=[
-            pltpu.VMEM((BEAMS, 2, 8, SIDE), F32),
-            pltpu.VMEM((GROUP, BEAMS, 2, 8, SIDE), F32),
-            pltpu.VMEM((3, BEAMS, SIDE), F32),
-            pltpu.VMEM((3, BEAMS, SIDE), F32),
+            pltpu.VMEM((1, SLOTS, SIDE), jnp.int32),
+            pltpu.VMEM((1, SLOTS, SIDE), F32),
+            pltpu.VMEM((1, SLOTS, SIDE), F32),
+            pltpu.SMEM((1,), jnp.int32),
+            pltpu.SMEM((1,), jnp.int32),
+            pltpu.VMEM((1, SIDE), F32),
+            pltpu.VMEM((BEAMS, 2, TIME_SLOTS // GROUP), F32),
+            pltpu.VMEM((SIDE_AZ, SIDE_AZ, BEAMS, 2, 8, SIDE), F32),
+            pltpu.VMEM((3, SLOTS, SIDE), F32),
+            pltpu.VMEM((3, SLOTS, SIDE), F32),
             pltpu.VMEM((BEAMS, 2 * SIDE, 2 * SIDE), F32),
             pltpu.VMEM((2, 2 * SIDE, 2 * SIDE), BF16),
             pltpu.VMEM((2, 2 * SIDE, 2 * SIDE), BF16),
@@ -312,12 +375,13 @@
             pltpu.VMEM((SIDE, 2 * SIDE), BF16),
             pltpu.VMEM((GROUP * BEAMS * 8, SIDE), F32),
             pltpu.VMEM((GROUP * BEAMS * 8, SIDE), F32),
-            dma, dma((BEAMS // chunk,)), dma, dma, dma, dma,
+            dma((7,)), dma, dma((BEAMS,)), dma, dma((BEAMS,)), dma, dma, dma, dma,
+            pltpu.SemaphoreType.REGULAR,
         ],
         compiler_params=pltpu.CompilerParams(
             collective_id=0, has_side_effects=True, vmem_limit_bytes=40 * 1024 * 1024
         ),
-    )(*arrays)
+    )(lag, frac, amp, offset, count, ambient.reshape(1, SIDE), pulse)
 
 
 def solution(mesh):

time: 38.8 us -> 36.4 us (0.938)
  Pallas kernels: 34.3 us -> 31.8 us
    pallas_call x1, Pallas kernels: 34.3 us -> 31.8 us  [per_device(): pl.pallas_call(kernel, out_shape=jax.ShapeDtypeStruct((1, GROUP * BEAMS,...]
    unnamed x12 -> x11, local copies, waits for them, and re-layouts: 2.93 us -> 2.99 us
where the time goes in v1:
time: 36.4 us; the launch traced here: 36.2 us
  Pallas kernels  31.8 us (87%)
  local copies, waits for them, and re-layouts  2.99 us (8%)
  between operations  1.35 us (4%)
    pallas_call x1, Pallas kernels, per_device(): pl.pallas_call(kernel, out_shape=jax.ShapeDtypeStruct((1, GROUP * BEAMS,...  31.8 us
    unnamed x11, local copies, waits for them, and re-layouts  2.99 us

profile of v1, /device:TPU:1, one launch (start us, length us, event | category | flops | bytes accessed | tf_op | source)
XLA Modules:
  0.0 36.2 jit_solution(2049452541737017150)
XLA Ops:
  0.7 0.0 copy-start.2
  1.3 0.0 copy-start.1
  1.3 0.0 copy-start.4
  1.3 0.0 copy-done.2
  1.4 0.7 %copy-done.1 = s32[1,128,8]{1,2,0:T(8,128)S(1)} copy-done((s32[1,128,8]{1,2,0:T(8,128)S(1)}, s32[1,128,8]{1,2,0:T(8,128)}, u32[]{:S(2)}) %copy-start.1) | copy-done | bytes 4120
  2.0 0.0 copy-done.4
  2.0 0.0 copy-start
  2.0 0.8 %copy-done = f32[8,2,1024]{2,1,0:T(2,128)S(1)} copy-done((f32[8,2,1024]{2,1,0:T(2,128)S(1)}, f32[8,2,1024]{2,1,0:T(2,128)}, u32[]{:S(2)}) %copy-start) | copy-done | bytes 65560
  2.9 0.0 copy-start.3
  2.9 0.7 %copy-done.3 = f32[1,128,8]{1,2,0:T(8,128)S(1)} copy-done((f32[1,128,8]{1,2,0:T(8,128)S(1)}, f32[1,128,8]{1,2,0:T(8,128)}, u32[]{:S(2)}) %copy-start.3) | copy-done | bytes 4120
  3.5 31.8 %shard_map.73 = f32[1,128,1024]{2,1,0:T(8,128)S(1)} custom-call(s32[1,8,128]{2,1,0:T(8,128)S(1)} %bitcast.4, f32[1,8,128]{2,1,0:T(8,128)S(1)} %bitcast.5, f32[1,8,128]{2,1,0:T(8,128)S(1)} %bitcast.6, s32[1]{0:T(128)S(6)} %copy.9.offset_hbm, s32[1]{0:T(128)S(6)} %copy.10.count_hbm, f32[1,128]{1,0:T(1,128)S(1)} %bitcast.7, f32[8,2,1024]{2,1,0:T(2,128)S(1)} %copy-done), custom_call_target="tpu_custom_call" | custom-call | tf_op jit(solution)/shard_map/pallas_call | solution.py:354
  35.4 0.8 %copy.11 = f32[1,128,1024]{2,1,0:T(8,128)} copy(f32[1,128,1024]{2,1,0:T(8,128)S(1)} %shard_map.73) | data formatting | bytes 1048576
Async XLA Ops:
  0.7 0.7 %copy-start.2 = (f32[1,128,8]{1,2,0:T(8,128)S(1)}, f32[1,128,8]{1,2,0:T(8,128)}, u32[]{:S(2)}) copy-start(f32[1,128,8]{1,2,0:T(8,128)} %param.8) | copy-start | bytes 12292
  1.3 0.7 %copy-start.1 = (s32[1,128,8]{1,2,0:T(8,128)S(1)}, s32[1,128,8]{1,2,0:T(8,128)}, u32[]{:S(2)}) copy-start(s32[1,128,8]{1,2,0:T(8,128)} %param.7) | copy-start | bytes 12292
  1.3 0.7 %copy-start.4 = (f32[128]{0:T(128)S(1)}, f32[128]{0:T(128)}, u32[]{:S(2)}) copy-start(f32[128]{0:T(128)} %param.12) | copy-start | bytes 1540
  2.0 0.8 %copy-start = (f32[8,2,1024]{2,1,0:T(2,128)S(1)}, f32[8,2,1024]{2,1,0:T(2,128)}, u32[]{:S(2)}) copy-start(f32[8,2,1024]{2,1,0:T(2,128)} %pulse_hbm.1) | copy-start | bytes 196612
  2.9 0.7 %copy-start.3 = (f32[1,128,8]{1,2,0:T(8,128)S(1)}, f32[1,128,8]{1,2,0:T(8,128)}, u32[]{:S(2)}) copy-start(f32[1,128,8]{1,2,0:T(8,128)} %param.9) | copy-start | bytes 12292

commit v2 on v1

v2 whole, which is shorter than its diff:
```python
import math

import jax
import jax.numpy as jnp
from jax import lax
from jax.experimental import pallas as pl
from jax.experimental.pallas import tpu as pltpu
from jax.sharding import PartitionSpec as P

TIME_SLOTS = 16384
SIDE = 128
BEAMS = 8
SLOTS = 8
GROUP = 16
HALF = 8
EXTRA = 4
TOGETHER = 4
ALL = BEAMS + EXTRA
EARLY_ORDER = (1, 0, 7, 6, 3, 2, 5, 4)
SIDE_AZ = 4
MESH = pl.DeviceIdType.MESH
F32 = jnp.float32
BF16 = jnp.bfloat16


def iota(shape, dim):
    return lax.broadcasted_iota(jnp.int32, shape, dim)


def cos_sin(turns):
    x = (turns - jnp.round(turns)) * math.pi
    y = x * x
    s = -1.0 / 39916800 * y + 1.0 / 362880
    s = s * y - 1.0 / 5040
    s = s * y + 1.0 / 120
    s = s * y - 1.0 / 6
    s = (s * y + 1.0) * x
    c = 1.0 / 479001600 * y - 1.0 / 3628800
    c = c * y + 1.0 / 40320
    c = c * y - 1.0 / 720
    c = c * y + 1.0 / 24
    c = c * y - 0.5
    c = c * y + 1.0
    return 1.0 - 2.0 * s * s, 2.0 * s * c


def split(x):
    hi = x.astype(BF16)
    return hi, (x - hi.astype(F32)).astype(BF16)


def dot(a, b):
    return jnp.dot(a, b, preferred_element_type=F32)


def dot3(a_hi, a_lo, b_hi, b_lo):
    return dot(a_hi, b_hi) + dot(a_hi, b_lo) + dot(a_lo, b_hi)


def blocks(a, b, c, d):
    return jnp.concatenate(
        [jnp.concatenate([a, b], axis=1), jnp.concatenate([c, d], axis=1)], axis=0
    )


def dft_tables():
    row, col = iota((SIDE, SIDE), 0), iota((SIDE, SIDE), 1)
    c, s = cos_sin(((row * col) & (SIDE - 1)).astype(F32) * (1.0 / SIDE))
    left = split(blocks(c, -s, s, c))
    right = split(blocks(c, s, -s, c))
    twist = cos_sin((row * col).astype(F32) * (1.0 / TIME_SLOTS))
    return left, right, twist


def prefix_tables():
    row, col = iota((SIDE, SIDE), 0), iota((SIDE, SIDE), 1)
    upper = jnp.where(row < col, 1.0, 0.0).astype(F32)
    ones = jnp.ones((SIDE, SIDE), F32)
    lower = jnp.where(col < row, 1.0, 0.0).astype(F32)
    inner = blocks(upper, ones, upper, ones).astype(BF16)
    outer = jnp.concatenate([lower, lower], axis=1).astype(BF16)
    return inner, outer


def as_column(near, far, shift):
    rows = jnp.concatenate([near, far] * BEAMS, axis=0)
    row, col = iota((SIDE, SIDE), 0), iota((SIDE, SIDE), 1)
    return jnp.sum(jnp.where((row >> 4) + shift == col, rows, 0.0), axis=1, keepdims=True)


def as_row(column):
    row, col = iota((SIDE, SIDE), 0), iota((SIDE, SIDE), 1)
    wide = jnp.broadcast_to(column, (SIDE, SIDE))
    return jnp.sum(jnp.where(row == col, wide, 0.0), axis=0, keepdims=True)


def phase_tables(near, far, shift=0):
    delay, frac, amp = [as_column(n, f, shift) for n, f in zip(near, far)]
    row, col = iota((SIDE, SIDE), 0), iota((SIDE, SIDE), 1)
    whole = (col * delay.astype(jnp.int32)) & (TIME_SLOTS - 1)
    inner_c, inner_s = cos_sin((whole.astype(F32) + col.astype(F32) * frac) * (1.0 / TIME_SLOTS))
    inner_c, inner_s = inner_c * amp, inner_s * amp
    near_row = (row & SLOTS) == 0
    parts = []
    for x in (inner_c, inner_s):
        parts.append(
            jnp.concatenate([jnp.where(near_row, x, 0.0), jnp.where(near_row, 0.0, x)], axis=1)
        )
    right = split(jnp.concatenate(parts, axis=0))
    signed = row - jnp.where(row >= SIDE // 2, SIDE, 0)
    whole = (signed * as_row(delay).astype(jnp.int32)) & (SIDE - 1)
    outer_c, outer_s = cos_sin((whole.astype(F32) + signed.astype(F32) * as_row(frac)) * (1.0 / SIDE))
    left = split(blocks(outer_c, -outer_s, -outer_s, -outer_c))
    return left, right


def spectrum(left, right, beam):
    mine = ((iota((2 * SIDE, 2 * SIDE), 0) & (SIDE - 1)) >> 4) == beam
    hi, lo = [jnp.where(mine, x.astype(F32), 0.0).astype(BF16) for x in right]
    return dot3(left[0], left[1], hi, lo)


def side_by_side(*parts):
    return jnp.concatenate(parts, axis=1)


def stacked(*parts):
    return jnp.concatenate(parts, axis=0)


def group_histogram(specs, pulses, ambients, left, right, twist, inner, outer):
    count = len(specs)
    rows = []
    for spec, (pulse_real, pulse_imag) in zip(specs, pulses):
        real, imag = spec[:SIDE], spec[SIDE:]
        wide_real, wide_imag = side_by_side(pulse_real, pulse_real), side_by_side(pulse_imag, pulse_imag)
        hi, lo = split(stacked(wide_real * real - wide_imag * imag, wide_real * imag + wide_imag * real))
        section = dot(left, stacked(hi, lo, hi))
        for trip in range(2):
            real = section[:SIDE, trip * SIDE : (trip + 1) * SIDE]
            imag = section[SIDE:, trip * SIDE : (trip + 1) * SIDE]
            rows.append(side_by_side(real * twist[0] - imag * twist[1], real * twist[1] + imag * twist[0]))
    hi, lo = split(stacked(*rows))
    field = dot(side_by_side(hi, lo, hi), right)
    fluxes = []
    for j in range(count):
        power = field[2 * SIDE * j : 2 * SIDE * (j + 1)]
        power = power * power
        power = power[:SIDE] + power[SIDE:]
        power = power[:, :SIDE] + power[:, SIDE:]
        fluxes.append(jnp.transpose((power * (1.0 / TIME_SLOTS) + ambients[j]) * (1.0 / TIME_SLOTS)))
    flux = stacked(*fluxes)
    hi, lo = split(flux)
    sums = dot(side_by_side(hi, lo), inner)
    hi, lo = split(side_by_side(*[sums[SIDE * j : SIDE * (j + 1), SIDE:] for j in range(count)]))
    carried = dot(outer, stacked(hi, lo))
    before = stacked(
        *[sums[SIDE * j : SIDE * (j + 1), :SIDE] + carried[:, SIDE * j : SIDE * (j + 1)] for j in range(count)]
    )
    series = 1.0 - flux * 0.25
    series = 1.0 - flux * (1.0 / 3) * series
    series = 1.0 - flux * 0.5 * series
    detected = jnp.where(flux < 1.0 / 32, flux * series, 1.0 - jnp.exp(-flux))
    return TIME_SLOTS * detected * jnp.exp(-before)


def kernel(
    lag_hbm, frac_hbm, amp_hbm, packed_hbm, ambient_hbm, pulse_hbm,
    out_ref,
    lag_ref, frac_ref, amp_ref, packed_ref, ambient_ref, pulse_ref,
    gathered, echo_out, echo_in, spec, left_tab, right_tab, twist_tab, inner_tab, outer_tab,
    ready, arrived,
    in_sem, shard_send, shard_recv, first_send, first_recv, second_send, second_recv, echo_send, echo_recv,
    hist_send, hist_recv, go_sem,
):
    me_range, me_az = lax.axis_index("range"), lax.axis_index("az")
    y, x = me_az // SIDE_AZ, lax.rem(me_az, SIDE_AZ)
    chief = GROUP - 1
    early = me_range < HALF
    late = jnp.logical_not(early)
    partner = lax.rem(me_range + HALF, GROUP)

    def row_peer(k):
        return y * SIDE_AZ + lax.rem(x + k, SIDE_AZ)

    def column_peer(k):
        return lax.rem(y + k, SIDE_AZ) * SIDE_AZ + x

    def remote(src, dst, send, recv, **where):
        return pltpu.make_async_remote_copy(
            src_ref=src, dst_ref=dst, send_sem=send, recv_sem=recv, device_id=where, device_id_type=MESH
        )

    fetches = [
        pltpu.make_async_copy(src, dst, in_sem.at[i])
        for i, (src, dst) in enumerate(
            (
                (pulse_hbm, pulse_ref), (lag_hbm, lag_ref), (frac_hbm, frac_ref), (amp_hbm, amp_ref),
                (packed_hbm, packed_ref), (ambient_hbm, ambient_ref),
            )
        )
    ]
    for fetch in fetches:
        fetch.start()

    barrier = pltpu.get_barrier_semaphore()
    for k in range(1, SIDE_AZ):
        for peer in (row_peer(k), column_peer(k)):
            pl.semaphore_signal(barrier, inc=1, device_id={"az": peer}, device_id_type=MESH)
    pl.semaphore_signal(
        barrier, inc=1, device_id={"az": lax.rem(me_az + GROUP - 1, GROUP)}, device_id_type=MESH
    )

    @pl.when(me_range != chief)
    def _():
        pl.semaphore_signal(barrier, inc=1, device_id={"range": chief}, device_id_type=MESH)

    @pl.when(early)
    def _():
        pl.semaphore_signal(barrier, inc=1, device_id={"range": partner}, device_id_type=MESH)

    fetches[0].wait()
    for b in range(BEAMS):
        for part in range(2):
            for q in range(8):
                gathered[y, x, b, part, q : q + 1, :] = pulse_ref[
                    b, part : part + 1, q * SIDE : (q + 1) * SIDE
                ]
    for fetch in fetches[1:]:
        fetch.wait()
    back = lax.rem(SIDE - me_range * BEAMS, SIDE)
    delay = (lag_ref[0] + (packed_ref[...] >> 4)).astype(F32)
    live = iota((SLOTS, SIDE), 0) < (packed_ref[...] & 15)
    near_trip = delay < TIME_SLOTS
    amp = amp_ref[0]
    near_amp = jnp.where(live & near_trip, amp, 0.0)
    far_amp = jnp.where(live & jnp.logical_not(near_trip), amp, 0.0)
    delay, frac, near_amp, far_amp = [
        pltpu.roll(v, back, 1) for v in (delay, frac_ref[0], near_amp, far_amp)
    ]
    echo_out[0] = delay
    echo_out[1] = frac
    echo_out[2] = far_amp
    echo_out[3] = near_amp

    greeted = 2 * SIDE_AZ - 1
    pl.semaphore_wait(
        barrier,
        greeted + jnp.where(early, 0, 1) + jnp.where(me_range == chief, GROUP - 1, 0),
    )

    shard = remote(
        gathered.at[y, x, pl.ds(BEAMS - EXTRA, EXTRA)], gathered.at[y, x, pl.ds(BEAMS, EXTRA)],
        shard_send, shard_recv, range=partner,
    )
    pl.when(late)(shard.start)

    echo_copy = remote(
        echo_out.at[pl.ds(0, 3)], echo_in, echo_send, echo_recv, az=lax.rem(me_az + 1, GROUP)
    )
    echo_copy.start()

    def first_step(pair, carry):
        b = 2 * pair
        for k in (1, 3, 2):
            mine = gathered.at[y, x, b]
            remote(mine, mine, first_send, first_recv.at[b], az=row_peer(k)).start()
            mine = gathered.at[y, x, b + 1]
            remote(mine, mine, first_send, first_recv.at[b + 1], az=column_peer(k)).start()
        return carry

    lax.fori_loop(0, BEAMS // 2, first_step, 0)

    @pl.when(me_range == chief)
    def _():
        def tell(k, carry):
            pl.semaphore_signal(go_sem, inc=1, device_id={"range": k}, device_id_type=MESH)
            return carry

        lax.fori_loop(0, GROUP - 1, tell, 0)

    left, right, twist = dft_tables()
    left_tab[...] = side_by_side(left[0], left[0], left[1])
    right_tab[...] = stacked(right[0], right[0], right[1])
    twist_tab[0], twist_tab[1] = twist
    inner_tab[...], outer_tab[...] = prefix_tables()

    def second_step(pair, carry):
        b = 2 * pair
        for j in range(2):
            three = gathered.at[0, pl.ds(0, SIDE_AZ - 1), b + j]
            remote(three, three, first_send, first_recv.at[b + j], az=me_az).wait_recv()
        for k in (1, 3, 2):
            row = gathered.at[y, :, b]
            remote(row, row, second_send, second_recv.at[b], az=column_peer(k)).start()
            column = gathered.at[:, x, b + 1]
            remote(column, column, second_send, second_recv.at[b + 1], az=row_peer(k)).start()
        return carry

    lax.fori_loop(0, BEAMS // 2, second_step, 0)

    echo_copy.wait_recv()

    def spectra(shift, beams, place):
        near = (echo_out[0], echo_out[1], echo_out[3])
        far = (echo_in[0], echo_in[1], echo_in[2])
        echo_left, echo_right = phase_tables(near, far, shift)
        for i, b in enumerate(beams):
            spec[place + i] = spectrum(echo_left, echo_right, b)

    spectra(0, range(BEAMS), 0)

    @pl.when(early)
    def _():
        spectra(HALF * BEAMS, range(BEAMS - EXTRA, BEAMS), BEAMS)

    def tiles_of(row, count):
        return pl.ds(pl.multiple_of(row * 8, 8), count * 8)

    def tiles(ref, row, count):
        return ref.at[tiles_of(row, count)]

    def send_tiles(peer, b, row, count):
        @pl.when(peer != me_range)
        def _():
            remote(
                tiles(ready, peer * ALL + b, count), tiles(arrived, row, count),
                hist_send, hist_recv, range=peer,
            ).start()

    def work(group, carry):
        b0 = group * TOGETHER
        own = group * TOGETHER < BEAMS
        row = me_range * BEAMS + jnp.where(own, b0, b0 - EXTRA + HALF * BEAMS)
        specs, pulses, ambients = [], [], []
        for j in range(TOGETHER):
            twelve = gathered.at[pl.ds(0, SIDE_AZ - 1), :, b0 + j]
            remote(twelve, twelve, second_send, second_recv.at[b0 + j], az=me_az).wait_recv()
        for j in range(TOGETHER):
            specs.append(spec[b0 + j])
            pulses.append([gathered[:, :, b0 + j, part].reshape(SIDE, SIDE) for part in range(2)])
            mine = iota((1, SIDE), 1) == row + j
            ambients.append(jnp.sum(jnp.where(mine, ambient_ref[...], 0.0), axis=1, keepdims=True))
        hist = group_histogram(
            specs, pulses, ambients, left_tab[...], right_tab[...], (twist_tab[0], twist_tab[1]),
            inner_tab[...], outer_tab[...],
        )
        for j in range(TOGETHER):
            for g in range(GROUP):
                ready[pl.ds(pl.multiple_of((g * ALL + b0 + j) * 8, 8), 8), :] = hist[
                    j * SIDE + g * 8 : j * SIDE + (g + 1) * 8
                ]

        @pl.when((group == 0) & (me_range != chief))
        def _():
            pl.semaphore_wait(go_sem, 1)

        @pl.when(early | (b0 < BEAMS - EXTRA))
        def _():
            for peer in EARLY_ORDER:
                send_tiles(peer, b0, row, TOGETHER)

        @pl.when(b0 == BEAMS - TOGETHER)
        def _():
            def send(peer, carry):
                send_tiles(peer, 0, me_range * BEAMS, BEAMS)
                return carry

            lax.fori_loop(HALF, GROUP, send, 0)

        @pl.when(early & (group == 0))
        def _():
            shard.wait_recv()
            lax.fori_loop(BEAMS // 2, ALL // 2, first_step, 0)

        @pl.when(early & (group == 1))
        def _():
            lax.fori_loop(BEAMS // 2, ALL // 2, second_step, 0)

        return carry

    lax.fori_loop(0, jnp.where(early, ALL // TOGETHER, BEAMS // TOGETHER), work, 0)

    arrived[tiles_of(me_range * BEAMS, BEAMS), :] = ready[tiles_of(me_range * ALL, BEAMS), :]

    @pl.when(early)
    def _():
        arrived[tiles_of(partner * BEAMS + BEAMS - EXTRA, EXTRA), :] = ready[
            tiles_of(me_range * ALL + BEAMS, EXTRA), :
        ]

    def settled(ref, send, recv, count):
        some = tiles(ref, 0, count)
        return remote(some, some, send, recv, az=me_az)

    @pl.when(early)
    def _():
        settled(arrived, hist_send, hist_recv, GROUP * BEAMS - ALL).wait_recv()

    @pl.when(late)
    def _():
        settled(arrived, hist_send, hist_recv, GROUP * BEAMS - BEAMS).wait_recv()

    for g in range(GROUP):
        for s in range(8):
            out_ref[0, g * 8 : (g + 1) * 8, s * SIDE : (s + 1) * SIDE] = arrived[
                pl.ds(g * 64 + s, 8, stride=8), :
            ]
    @pl.when(early)
    def _():
        settled(ready, hist_send, hist_recv, (GROUP - 1) * BEAMS + (HALF - 1) * EXTRA).wait_send()

    @pl.when(late)
    def _():
        settled(ready, hist_send, hist_recv, (GROUP - 1) * BEAMS - HALF * EXTRA).wait_send()
        shard.wait_send()

    echo_copy.wait_send()

    def sent(beams):
        three = gathered.at[0, pl.ds(0, SIDE_AZ - 1), beams]
        remote(three, three, first_send, first_recv.at[0], az=me_az).wait_send()
        twelve = gathered.at[pl.ds(0, SIDE_AZ - 1), :, beams]
        remote(twelve, twelve, second_send, second_recv.at[0], az=me_az).wait_send()

    sent(pl.ds(0, BEAMS))

    @pl.when(early)
    def _():
        sent(pl.ds(BEAMS, EXTRA))


def per_device(lag, frac, amp, offset, count, ambient, pulse):
    lag, frac, amp = [jnp.swapaxes(v, 1, 2) for v in (lag, frac, amp)]
    hbm = pl.BlockSpec(memory_space=pltpu.HBM)
    dma = pltpu.SemaphoreType.DMA
    return pl.pallas_call(
        kernel,
        out_shape=jax.ShapeDtypeStruct((1, GROUP * BEAMS, TIME_SLOTS // GROUP), F32),
        in_specs=[hbm] * 6,
        out_specs=pl.BlockSpec(memory_space=pltpu.VMEM),
        scratch_shapes=[
            pltpu.VMEM((1, SLOTS, SIDE), jnp.int32),
            pltpu.VMEM((1, SLOTS, SIDE), F32),
            pltpu.VMEM((1, SLOTS, SIDE), F32),
            pltpu.VMEM((1, 1), jnp.int32),
            pltpu.VMEM((1, SIDE), F32),
            pltpu.VMEM((BEAMS, 2, TIME_SLOTS // GROUP), F32),
            pltpu.VMEM((SIDE_AZ, SIDE_AZ, ALL, 2, 8, SIDE), F32),
            pltpu.VMEM((4, SLOTS, SIDE), F32),
            pltpu.VMEM((3, SLOTS, SIDE), F32),
            pltpu.VMEM((ALL, 2 * SIDE, 2 * SIDE), F32),
            pltpu.VMEM((2 * SIDE, 6 * SIDE), BF16),
            pltpu.VMEM((6 * SIDE, 2 * SIDE), BF16),
            pltpu.VMEM((2, SIDE, SIDE), F32),
            pltpu.VMEM((2 * SIDE, 2 * SIDE), BF16),
            pltpu.VMEM((SIDE, 2 * SIDE), BF16),
            pltpu.VMEM((GROUP * ALL * 8, SIDE), F32),
            pltpu.VMEM((GROUP * BEAMS * 8, SIDE), F32),
            dma((6,)), dma, dma, dma, dma((ALL,)), dma, dma((ALL,)), dma, dma, dma, dma,
            pltpu.SemaphoreType.REGULAR,
        ],
        compiler_params=pltpu.CompilerParams(
            collective_id=0, has_side_effects=True, vmem_limit_bytes=40 * 1024 * 1024
        ),
    )(lag, frac, amp, (offset * 16 + count).reshape(1, 1), ambient.reshape(1, SIDE), pulse)


def solution(mesh):
    in_specs = (
        P("az", None, None),
        P("az", None, None),
        P("az", None, None),
        P("az"),
        P("az"),
        P(),
        P("range", None, "az"),
    )
    out_specs = P("az", None, "range")
    return jax.shard_map(
        per_device, mesh=mesh, in_specs=in_specs, out_specs=out_specs, check_vma=False
    )
```

time: 36.4 us -> 36.5 us (level)
  Pallas kernels: 31.8 us -> 32.6 us
  local copies, waits for them, and re-layouts: 2.99 us -> 2.32 us
    pallas_call x1, Pallas kernels: 31.8 us -> 32.6 us  [per_device(): pl.pallas_call(kernel, out_shape=jax.ShapeDtypeStruct((1, GROUP * BEAMS,...]
    unnamed x11, local copies, waits for them, and re-layouts: 2.99 us -> 2.32 us
where the time goes in v2:
time: 36.5 us; the launch traced here: 36.3 us
  Pallas kernels  32.6 us (89%)
  local copies, waits for them, and re-layouts  2.32 us (6%)
  between operations  1.34 us (4%)
    pallas_call x1, Pallas kernels, per_device(): pl.pallas_call(kernel, out_shape=jax.ShapeDtypeStruct((1, GROUP * BEAMS,...  32.6 us
    unnamed x11, local copies, waits for them, and re-layouts  2.32 us

profile of v2, /device:TPU:1, one launch (start us, length us, event | category | flops | bytes accessed | tf_op | source)
XLA Modules:
  0.0 36.3 jit_solution(5255531584069875020)
XLA Ops:
  1.3 0.0 copy-start.3
  1.3 0.0 copy-start.2
  1.3 0.0 copy-start.1
  1.3 0.0 copy-start.4
  1.3 0.6 %copy-done.3 = f32[1,128,8]{1,2,0:T(8,128)S(1)} copy-done((f32[1,128,8]{1,2,0:T(8,128)S(1)}, f32[1,128,8]{1,2,0:T(8,128)}, u32[]{:S(2)}) %copy-start.3) | copy-done | bytes 4120
  2.0 0.0 copy-done.2
  2.0 0.0 copy-done.1
  2.0 0.0 copy-done.4
  2.0 0.0 copy-start
  2.0 0.8 %copy-done = f32[8,2,1024]{2,1,0:T(2,128)S(1)} copy-done((f32[8,2,1024]{2,1,0:T(2,128)S(1)}, f32[8,2,1024]{2,1,0:T(2,128)}, u32[]{:S(2)}) %copy-start) | copy-done | bytes 65560
  2.9 32.6 %shard_map.73 = f32[1,128,1024]{2,1,0:T(8,128)S(1)} custom-call(s32[1,8,128]{2,1,0:T(8,128)S(1)} %bitcast.5, f32[1,8,128]{2,1,0:T(8,128)S(1)} %bitcast.6, f32[1,8,128]{2,1,0:T(8,128)S(1)} %bitcast.7, s32[1,1]{1,0:T(1,128)} %bitcast.3.packed_hbm, f32[1,128]{1,0:T(1,128)S(1)} %bitcast.8, f32[8,2,1024]{2,1,0:T(2,128)S(1)} %copy-done), custom_call_target="tpu_custom_call" | custom-call | tf_op jit(solution)/shard_map/pallas_call | solution.py:437
  35.5 0.8 %copy.11 = f32[1,128,1024]{2,1,0:T(8,128)} copy(f32[1,128,1024]{2,1,0:T(8,128)S(1)} %shard_map.73) | data formatting | bytes 1048576
Async XLA Ops:
  1.3 0.7 %copy-start.3 = (f32[1,128,8]{1,2,0:T(8,128)S(1)}, f32[1,128,8]{1,2,0:T(8,128)}, u32[]{:S(2)}) copy-start(f32[1,128,8]{1,2,0:T(8,128)} %param.9) | copy-start | bytes 12292
  1.3 0.7 %copy-start.2 = (f32[1,128,8]{1,2,0:T(8,128)S(1)}, f32[1,128,8]{1,2,0:T(8,128)}, u32[]{:S(2)}) copy-start(f32[1,128,8]{1,2,0:T(8,128)} %param.8) | copy-start | bytes 12292
  1.3 0.7 %copy-start.1 = (s32[1,128,8]{1,2,0:T(8,128)S(1)}, s32[1,128,8]{1,2,0:T(8,128)}, u32[]{:S(2)}) copy-start(s32[1,128,8]{1,2,0:T(8,128)} %param.7) | copy-start | bytes 12292
  1.3 0.7 %copy-start.4 = (f32[128]{0:T(128)S(1)}, f32[128]{0:T(128)}, u32[]{:S(2)}) copy-start(f32[128]{0:T(128)} %param.12) | copy-start | bytes 1540
  2.0 0.8 %copy-start = (f32[8,2,1024]{2,1,0:T(2,128)S(1)}, f32[8,2,1024]{2,1,0:T(2,128)}, u32[]{:S(2)}) copy-start(f32[8,2,1024]{2,1,0:T(2,128)} %pulse_hbm.1) | copy-start | bytes 196612

commit v3 on v2

v3 whole, which is shorter than its diff:
```python
import math

import jax
import jax.numpy as jnp
from jax import lax
from jax.experimental import pallas as pl
from jax.experimental.pallas import tpu as pltpu
from jax.sharding import PartitionSpec as P

TIME_SLOTS = 16384
SIDE = 128
BEAMS = 8
SLOTS = 8
GROUP = 16
EARLY_ORDER = (1, 0, 7, 6, 3, 2, 5, 4)
LATE_ORDER = (8, 9, 14, 15, 10, 11, 12, 13)
SIDE_AZ = 4
MESH = pl.DeviceIdType.MESH
F32 = jnp.float32
BF16 = jnp.bfloat16


def iota(shape, dim):
    return lax.broadcasted_iota(jnp.int32, shape, dim)


def cos_sin(turns):
    x = (turns - jnp.round(turns)) * math.pi
    y = x * x
    s = -1.0 / 39916800 * y + 1.0 / 362880
    s = s * y - 1.0 / 5040
    s = s * y + 1.0 / 120
    s = s * y - 1.0 / 6
    s = (s * y + 1.0) * x
    c = 1.0 / 479001600 * y - 1.0 / 3628800
    c = c * y + 1.0 / 40320
    c = c * y - 1.0 / 720
    c = c * y + 1.0 / 24
    c = c * y - 0.5
    c = c * y + 1.0
    return 1.0 - 2.0 * s * s, 2.0 * s * c


def split(x):
    hi = x.astype(BF16)
    return hi, (x - hi.astype(F32)).astype(BF16)


def dot(a, b):
    return jnp.dot(a, b, preferred_element_type=F32)


def dot3(a_hi, a_lo, b_hi, b_lo):
    return dot(a_hi, b_hi) + dot(a_hi, b_lo) + dot(a_lo, b_hi)


def blocks(a, b, c, d):
    return jnp.concatenate(
        [jnp.concatenate([a, b], axis=1), jnp.concatenate([c, d], axis=1)], axis=0
    )


def dft_tables():
    row, col = iota((SIDE, SIDE), 0), iota((SIDE, SIDE), 1)
    c, s = cos_sin(((row * col) & (SIDE - 1)).astype(F32) * (1.0 / SIDE))
    left = split(blocks(c, -s, s, c))
    right = split(blocks(c, s, -s, c))
    twist = cos_sin((row * col).astype(F32) * (1.0 / TIME_SLOTS))
    return left, right, twist


def prefix_tables():
    row, col = iota((SIDE, SIDE), 0), iota((SIDE, SIDE), 1)
    upper = jnp.where(row < col, 1.0, 0.0).astype(F32)
    ones = jnp.ones((SIDE, SIDE), F32)
    lower = jnp.where(col < row, 1.0, 0.0).astype(F32)
    inner = blocks(upper, ones, upper, ones).astype(BF16)
    outer = jnp.concatenate([lower, lower], axis=1).astype(BF16)
    return inner, outer


def as_column(rows, lane):
    return jnp.sum(jnp.where(iota(rows.shape, 1) == lane, rows, 0.0), axis=1, keepdims=True)


def as_row(column):
    row, col = iota((SIDE, SIDE), 0), iota((SIDE, SIDE), 1)
    wide = jnp.broadcast_to(column, (SIDE, SIDE))
    return jnp.sum(jnp.where(row == col, wide, 0.0), axis=0, keepdims=True)


def phase_tables(delay, frac, amp):
    row, col = iota((SIDE, SIDE), 0), iota((SIDE, SIDE), 1)
    whole = (col * delay.astype(jnp.int32)) & (TIME_SLOTS - 1)
    inner_c, inner_s = cos_sin((whole.astype(F32) + col.astype(F32) * frac) * (1.0 / TIME_SLOTS))
    inner_c, inner_s = inner_c * amp, inner_s * amp
    near_row = (row & SLOTS) == 0
    parts = []
    for x in (inner_c, inner_s):
        parts.append(
            jnp.concatenate([jnp.where(near_row, x, 0.0), jnp.where(near_row, 0.0, x)], axis=1)
        )
    right = split(jnp.concatenate(parts, axis=0))
    signed = row - jnp.where(row >= SIDE // 2, SIDE, 0)
    whole = (signed * as_row(delay).astype(jnp.int32)) & (SIDE - 1)
    outer_c, outer_s = cos_sin((whole.astype(F32) + signed.astype(F32) * as_row(frac)) * (1.0 / SIDE))
    left = split(blocks(outer_c, -outer_s, -outer_s, -outer_c))
    return left, right


def spectrum(left, right, beam):
    mine = ((iota((2 * SIDE, 2 * SIDE), 0) & (SIDE - 1)) >> 4) == beam
    hi, lo = [jnp.where(mine, x.astype(F32), 0.0).astype(BF16) for x in right]
    return dot3(left[0], left[1], hi, lo)


def side_by_side(*parts):
    return jnp.concatenate(parts, axis=1)


def stacked(*parts):
    return jnp.concatenate(parts, axis=0)


def group_histogram(specs, pulses, ambients, left, right, twist, inner, outer):
    count = len(specs)
    rows = []
    for spec, (pulse_real, pulse_imag) in zip(specs, pulses):
        real, imag = spec[:SIDE], spec[SIDE:]
        wide_real, wide_imag = side_by_side(pulse_real, pulse_real), side_by_side(pulse_imag, pulse_imag)
        hi, lo = split(stacked(wide_real * real - wide_imag * imag, wide_real * imag + wide_imag * real))
        section = dot(left, stacked(hi, lo, hi))
        for trip in range(2):
            real = section[:SIDE, trip * SIDE : (trip + 1) * SIDE]
            imag = section[SIDE:, trip * SIDE : (trip + 1) * SIDE]
            rows.append(side_by_side(real * twist[0] - imag * twist[1], real * twist[1] + imag * twist[0]))
    hi, lo = split(stacked(*rows))
    field = dot(side_by_side(hi, lo, hi), right)
    fluxes = []
    for j in range(count):
        power = field[2 * SIDE * j : 2 * SIDE * (j + 1)]
        power = power * power
        power = power[:SIDE] + power[SIDE:]
        power = power[:, :SIDE] + power[:, SIDE:]
        fluxes.append(jnp.transpose((power * (1.0 / TIME_SLOTS) + ambients[j]) * (1.0 / TIME_SLOTS)))
    flux = stacked(*fluxes)
    hi, lo = split(flux)
    sums = dot(side_by_side(hi, lo), inner)
    hi, lo = split(side_by_side(*[sums[SIDE * j : SIDE * (j + 1), SIDE:] for j in range(count)]))
    carried = dot(outer, stacked(hi, lo))
    before = stacked(
        *[sums[SIDE * j : SIDE * (j + 1), :SIDE] + carried[:, SIDE * j : SIDE * (j + 1)] for j in range(count)]
    )
    series = 1.0 - flux * 0.25
    series = 1.0 - flux * (1.0 / 3) * series
    series = 1.0 - flux * 0.5 * series
    detected = jnp.where(flux < 1.0 / 32, flux * series, 1.0 - jnp.exp(-flux))
    return TIME_SLOTS * detected * jnp.exp(-before)


def kernel(
    lag_hbm, frac_hbm, amp_hbm, packed_hbm, ambient_hbm, pulse_hbm,
    out_ref,
    lag_ref, frac_ref, amp_ref, packed_ref, ambient_ref, pulse_ref,
    own, gathered, echo_left, echo_right, left_tab, right_tab, twist_tab, inner_tab, outer_tab,
    ready, arrived,
    in_sem, pulse_send, pulse_recv, hist_send, hist_recv, go_sem, near_sem,
):
    me_range, me_az = lax.axis_index("range"), lax.axis_index("az")
    y, x = me_az // SIDE_AZ, lax.rem(me_az, SIDE_AZ)
    chief = GROUP - 1

    def remote(src, dst, send, recv, **where):
        return pltpu.make_async_remote_copy(
            src_ref=src, dst_ref=dst, send_sem=send, recv_sem=recv, device_id=where, device_id_type=MESH
        )

    fetches = [
        pltpu.make_async_copy(src, dst, in_sem.at[i])
        for i, (src, dst) in enumerate(
            (
                (pulse_hbm, pulse_ref), (lag_hbm, lag_ref), (frac_hbm, frac_ref), (amp_hbm, amp_ref),
                (packed_hbm, packed_ref), (ambient_hbm, ambient_ref),
            )
        )
    ]
    for fetch in fetches:
        fetch.start()

    barrier = pltpu.get_barrier_semaphore()

    def greet(k, carry):
        pl.semaphore_signal(
            barrier, inc=1, device_id={"az": lax.rem(me_az + k, GROUP)}, device_id_type=MESH
        )
        return carry

    lax.fori_loop(1, GROUP, greet, 0)

    @pl.when(me_range != chief)
    def _():
        pl.semaphore_signal(barrier, inc=1, device_id={"range": chief}, device_id_type=MESH)

    fetches[0].wait()
    for b in range(BEAMS):
        for part in range(2):
            for q in range(8):
                own[b, part, q : q + 1, :] = pulse_ref[b, part : part + 1, q * SIDE : (q + 1) * SIDE]
    for fetch in fetches[1:]:
        fetch.wait()
    first = me_range * BEAMS
    delay = (lag_ref[0] + (packed_ref[...] >> 4)).astype(F32)
    live = iota((SLOTS, SIDE), 0) < (packed_ref[...] & 15)
    amp = jnp.where(live, amp_ref[0], 0.0)
    delay, frac, amp = [
        pltpu.roll(v, lax.rem(2 * SIDE + BEAMS * i - first, SIDE), 1)
        for i, v in enumerate((delay, frac_ref[0], amp))
    ]
    lane = iota((SLOTS, SIDE), 1)
    echo = jnp.where(lane < BEAMS, delay, jnp.where(lane < 2 * BEAMS, frac, amp))
    for b in range(0, BEAMS, 2):
        own[b, 2] = echo

    pl.semaphore_wait(barrier, GROUP - 1 + jnp.where(me_range == chief, GROUP - 1, 0))

    def share(k, carry):
        peer = lax.rem(me_az + k, GROUP)
        beam = 2 * lax.rem(peer, SIDE_AZ)
        remote(own.at[beam], gathered.at[0, me_az], pulse_send, pulse_recv.at[0], az=peer).start()
        return carry

    def share_next(k, carry):
        peer = lax.rem(me_az + k, GROUP)
        beam = 2 * lax.rem(peer, SIDE_AZ) + 1
        parts = pl.ds(0, 2)
        remote(
            own.at[beam, parts], gathered.at[1, me_az, parts], pulse_send, pulse_recv.at[1], az=peer
        ).start()
        return carry

    lax.fori_loop(1, GROUP, share, 0)
    lax.fori_loop(1, GROUP, share_next, 0)

    @pl.when(me_range == chief)
    def _():
        def tell(k, carry):
            pl.semaphore_signal(go_sem, inc=1, device_id={"range": k}, device_id_type=MESH)
            return carry

        lax.fori_loop(0, GROUP - 1, tell, 0)

    gathered[0, me_az] = own[2 * x]
    gathered[1, me_az] = own[2 * x + 1]

    left, right, twist = dft_tables()
    left_tab[...] = side_by_side(left[0], left[0], left[1])
    right_tab[...] = stacked(right[0], right[0], right[1])
    twist_tab[0], twist_tab[1] = twist
    inner_tab[...], outer_tab[...] = prefix_tables()

    @pl.when(me_range != chief)
    def _():
        pl.semaphore_wait(go_sem, 1)

    for k in range(1, SIDE_AZ):
        pl.semaphore_signal(
            near_sem, inc=1, device_id={"az": y * SIDE_AZ + lax.rem(x + k, SIDE_AZ)}, device_id_type=MESH
        )

    some = gathered.at[0, pl.ds(0, GROUP - 1)]
    remote(some, some, pulse_send, pulse_recv.at[0], az=me_az).wait_recv()
    rows = []
    for i in range(SIDE_AZ):
        rows.append(gathered[0, y * SIDE_AZ + i, 2])
        rows.append(gathered[0, lax.rem(y * SIDE_AZ + i + GROUP - 1, GROUP), 2])
    rows = stacked(*(rows * 2))
    place = 2 * x + (iota((SIDE, SIDE), 0) >> 6)
    delay, frac, amp = [as_column(rows, place + BEAMS * i) for i in range(3)]
    far = (iota((SIDE, 1), 0) & SLOTS) != 0
    amp = jnp.where(far == (delay >= TIME_SLOTS), amp, 0.0)
    (echo_left[0], echo_left[1]), (echo_right[0], echo_right[1]) = phase_tables(delay, frac, amp)

    def tiles_of(row, count):
        return pl.ds(pl.multiple_of(row * 8, 8), count * 8)

    def tiles(ref, row, count):
        return ref.at[tiles_of(row, count)]

    def send_tile(j, i, peer):
        @pl.when((peer != me_range) | (i != x))
        def _():
            remote(
                tiles(ready, (j * SIDE_AZ + i) * GROUP + peer, 1),
                tiles(arrived, me_range * BEAMS + 2 * x + j, 1),
                hist_send, hist_recv, range=peer, az=y * SIDE_AZ + i,
            ).start()

    def send_tiles(j, order):
        def column(k, carry):
            i = lax.rem(x + k, SIDE_AZ)
            for peer in order:
                send_tile(j, i, peer)
            return carry

        lax.fori_loop(0, SIDE_AZ, column, 0)

    def work(j, carry):
        @pl.when(j == 1)
        def _():
            some = gathered.at[1, pl.ds(0, GROUP - 1), pl.ds(0, 2)]
            remote(some, some, pulse_send, pulse_recv.at[1], az=me_az).wait_recv()

        e_left, e_right = (echo_left[0], echo_left[1]), (echo_right[0], echo_right[1])
        specs = [spectrum(e_left, e_right, j * SIDE_AZ + i) for i in range(SIDE_AZ)]
        pulse = [gathered[j, :, part].reshape(SIDE, SIDE) for part in range(2)]
        mine = iota((1, SIDE), 1) == first + 2 * x + j
        ambient = jnp.sum(jnp.where(mine, ambient_ref[...], 0.0), axis=1, keepdims=True)
        hist = group_histogram(
            specs, [pulse] * SIDE_AZ, [ambient] * SIDE_AZ, left_tab[...], right_tab[...],
            (twist_tab[0], twist_tab[1]), inner_tab[...], outer_tab[...],
        )
        ready[tiles_of(j * SIDE_AZ * GROUP, SIDE_AZ * GROUP), :] = hist

        @pl.when(j == 0)
        def _():
            pl.semaphore_wait(near_sem, SIDE_AZ - 1)

        send_tiles(j, EARLY_ORDER)
        return carry

    lax.fori_loop(0, 2, work, 0)
    send_tiles(0, LATE_ORDER)
    send_tiles(1, LATE_ORDER)
    for j in range(2):
        arrived[tiles_of(me_range * BEAMS + 2 * x + j, 1), :] = ready[
            tiles_of((j * SIDE_AZ + x) * GROUP + me_range, 1), :
        ]

    some = tiles(arrived, 0, GROUP * BEAMS - 2)
    done = remote(some, some, hist_send, hist_recv, az=me_az)
    done.wait_recv()
    for g in range(GROUP):
        for s in range(8):
            out_ref[0, g * 8 : (g + 1) * 8, s * SIDE : (s + 1) * SIDE] = arrived[
                pl.ds(g * 64 + s, 8, stride=8), :
            ]
    done.wait_send()
    some = gathered.at[0, pl.ds(0, GROUP - 1)]
    remote(some, some, pulse_send, pulse_recv.at[0], az=me_az).wait_send()
    some = gathered.at[1, pl.ds(0, GROUP - 1), pl.ds(0, 2)]
    remote(some, some, pulse_send, pulse_recv.at[1], az=me_az).wait_send()


def per_device(lag, frac, amp, offset, count, ambient, pulse):
    lag, frac, amp = [jnp.swapaxes(v, 1, 2) for v in (lag, frac, amp)]
    hbm = pl.BlockSpec(memory_space=pltpu.HBM)
    dma = pltpu.SemaphoreType.DMA
    return pl.pallas_call(
        kernel,
        out_shape=jax.ShapeDtypeStruct((1, GROUP * BEAMS, TIME_SLOTS // GROUP), F32),
        in_specs=[hbm] * 6,
        out_specs=pl.BlockSpec(memory_space=pltpu.VMEM),
        scratch_shapes=[
            pltpu.VMEM((1, SLOTS, SIDE), jnp.int32),
            pltpu.VMEM((1, SLOTS, SIDE), F32),
            pltpu.VMEM((1, SLOTS, SIDE), F32),
            pltpu.VMEM((1, 1), jnp.int32),
            pltpu.VMEM((1, SIDE), F32),
            pltpu.VMEM((BEAMS, 2, TIME_SLOTS // GROUP), F32),
            pltpu.VMEM((BEAMS, 3, 8, SIDE), F32),
            pltpu.VMEM((2, GROUP, 3, 8, SIDE), F32),
            pltpu.VMEM((2, 2 * SIDE, 2 * SIDE), BF16),
            pltpu.VMEM((2, 2 * SIDE, 2 * SIDE), BF16),
            pltpu.VMEM((2 * SIDE, 6 * SIDE), BF16),
            pltpu.VMEM((6 * SIDE, 2 * SIDE), BF16),
            pltpu.VMEM((2, SIDE, SIDE), F32),
            pltpu.VMEM((2 * SIDE, 2 * SIDE), BF16),
            pltpu.VMEM((SIDE, 2 * SIDE), BF16),
            pltpu.VMEM((GROUP * BEAMS * 8, SIDE), F32),
            pltpu.VMEM((GROUP * BEAMS * 8, SIDE), F32),
            dma((6,)), dma, dma((2,)), dma, dma,
            pltpu.SemaphoreType.REGULAR, pltpu.SemaphoreType.REGULAR,
        ],
        compiler_params=pltpu.CompilerParams(
            collective_id=0, has_side_effects=True, vmem_limit_bytes=40 * 1024 * 1024
        ),
    )(lag, frac, amp, (offset * 16 + count).reshape(1, 1), ambient.reshape(1, SIDE), pulse)


def solution(mesh):
    in_specs = (
        P("az", None, None),
        P("az", None, None),
        P("az", None, None),
        P("az"),
        P("az"),
        P(),
        P("range", None, "az"),
    )
    out_specs = P("az", None, "range")
    return jax.shard_map(
        per_device, mesh=mesh, in_specs=in_specs, out_specs=out_specs, check_vma=False
    )
```

time: 36.5 us -> 35.2 us (0.964)
  Pallas kernels: 32.6 us -> 31.3 us
    pallas_call x1, Pallas kernels: 32.6 us -> 31.3 us  [per_device(): pl.pallas_call(kernel, out_shape=jax.ShapeDtypeStruct((1, GROUP * BEAMS,...]
where the time goes in v3:
time: 35.2 us; the launch traced here: 35 us
  Pallas kernels  31.3 us (89%)
  local copies, waits for them, and re-layouts  2.32 us (7%)
  between operations  1.34 us (4%)
    pallas_call x1, Pallas kernels, per_device(): pl.pallas_call(kernel, out_shape=jax.ShapeDtypeStruct((1, GROUP * BEAMS,...  31.3 us
    unnamed x11, local copies, waits for them, and re-layouts  2.32 us

profile of v3, /device:TPU:1, one launch (start us, length us, event | category | flops | bytes accessed | tf_op | source)
XLA Modules:
  0.0 35.0 jit_solution(8394406863799472768)
XLA Ops:
  1.3 0.0 copy-start.3
  1.3 0.0 copy-start.2
  1.3 0.0 copy-start.1
  1.3 0.0 copy-start.4
  1.3 0.6 %copy-done.3 = f32[1,128,8]{1,2,0:T(8,128)S(1)} copy-done((f32[1,128,8]{1,2,0:T(8,128)S(1)}, f32[1,128,8]{1,2,0:T(8,128)}, u32[]{:S(2)}) %copy-start.3) | copy-done | bytes 4120
  2.0 0.0 copy-done.2
  2.0 0.0 copy-done.1
  2.0 0.0 copy-done.4
  2.0 0.0 copy-start
  2.0 0.8 %copy-done = f32[8,2,1024]{2,1,0:T(2,128)S(1)} copy-done((f32[8,2,1024]{2,1,0:T(2,128)S(1)}, f32[8,2,1024]{2,1,0:T(2,128)}, u32[]{:S(2)}) %copy-start) | copy-done | bytes 65560
  2.9 31.3 %shard_map.73 = f32[1,128,1024]{2,1,0:T(8,128)S(1)} custom-call(s32[1,8,128]{2,1,0:T(8,128)S(1)} %bitcast.5, f32[1,8,128]{2,1,0:T(8,128)S(1)} %bitcast.6, f32[1,8,128]{2,1,0:T(8,128)S(1)} %bitcast.7, s32[1,1]{1,0:T(1,128)} %bitcast.3.packed_hbm, f32[1,128]{1,0:T(1,128)S(1)} %bitcast.8, f32[8,2,1024]{2,1,0:T(2,128)S(1)} %copy-done), custom_call_target="tpu_custom_call" | custom-call | tf_op jit(solution)/shard_map/pallas_call | solution.py:358
  34.2 0.8 %copy.11 = f32[1,128,1024]{2,1,0:T(8,128)} copy(f32[1,128,1024]{2,1,0:T(8,128)S(1)} %shard_map.73) | data formatting | bytes 1048576
Async XLA Ops:
  1.3 0.7 %copy-start.3 = (f32[1,128,8]{1,2,0:T(8,128)S(1)}, f32[1,128,8]{1,2,0:T(8,128)}, u32[]{:S(2)}) copy-start(f32[1,128,8]{1,2,0:T(8,128)} %param.9) | copy-start | bytes 12292
  1.3 0.7 %copy-start.2 = (f32[1,128,8]{1,2,0:T(8,128)S(1)}, f32[1,128,8]{1,2,0:T(8,128)}, u32[]{:S(2)}) copy-start(f32[1,128,8]{1,2,0:T(8,128)} %param.8) | copy-start | bytes 12292
  1.3 0.7 %copy-start.1 = (s32[1,128,8]{1,2,0:T(8,128)S(1)}, s32[1,128,8]{1,2,0:T(8,128)}, u32[]{:S(2)}) copy-start(s32[1,128,8]{1,2,0:T(8,128)} %param.7) | copy-start | bytes 12292
  1.3 0.7 %copy-start.4 = (f32[128]{0:T(128)S(1)}, f32[128]{0:T(128)}, u32[]{:S(2)}) copy-start(f32[128]{0:T(128)} %param.12) | copy-start | bytes 1540
  2.0 0.8 %copy-start = (f32[8,2,1024]{2,1,0:T(2,128)S(1)}, f32[8,2,1024]{2,1,0:T(2,128)}, u32[]{:S(2)}) copy-start(f32[8,2,1024]{2,1,0:T(2,128)} %pulse_hbm.1) | copy-start | bytes 196612

commit v4 on v3

--- a/solution.py
+++ b/solution.py
@@ -12,6 +12,7 @@
 BEAMS = 8
 SLOTS = 8
 GROUP = 16
+HALF = 8
 EARLY_ORDER = (1, 0, 7, 6, 3, 2, 5, 4)
 LATE_ORDER = (8, 9, 14, 15, 10, 11, 12, 13)
 SIDE_AZ = 4
@@ -50,10 +51,6 @@
     return jnp.dot(a, b, preferred_element_type=F32)
 
 
-def dot3(a_hi, a_lo, b_hi, b_lo):
-    return dot(a_hi, b_hi) + dot(a_hi, b_lo) + dot(a_lo, b_hi)
-
-
 def blocks(a, b, c, d):
     return jnp.concatenate(
         [jnp.concatenate([a, b], axis=1), jnp.concatenate([c, d], axis=1)], axis=0
@@ -90,28 +87,27 @@
 
 
 def phase_tables(delay, frac, amp):
+    delay, frac, amp = [jnp.concatenate([v, v], axis=0) for v in (delay, frac, amp)]
     row, col = iota((SIDE, SIDE), 0), iota((SIDE, SIDE), 1)
     whole = (col * delay.astype(jnp.int32)) & (TIME_SLOTS - 1)
-    inner_c, inner_s = cos_sin((whole.astype(F32) + col.astype(F32) * frac) * (1.0 / TIME_SLOTS))
-    inner_c, inner_s = inner_c * amp, inner_s * amp
+    c, s = cos_sin((whole.astype(F32) + col.astype(F32) * frac) * (1.0 / TIME_SLOTS))
+    inner = jnp.where(row < SIDE // 2, c, s) * amp
     near_row = (row & SLOTS) == 0
-    parts = []
-    for x in (inner_c, inner_s):
-        parts.append(
-            jnp.concatenate([jnp.where(near_row, x, 0.0), jnp.where(near_row, 0.0, x)], axis=1)
-        )
-    right = split(jnp.concatenate(parts, axis=0))
+    right = split(
+        jnp.concatenate([jnp.where(near_row, inner, 0.0), jnp.where(near_row, 0.0, inner)], axis=1)
+    )
     signed = row - jnp.where(row >= SIDE // 2, SIDE, 0)
     whole = (signed * as_row(delay).astype(jnp.int32)) & (SIDE - 1)
-    outer_c, outer_s = cos_sin((whole.astype(F32) + signed.astype(F32) * as_row(frac)) * (1.0 / SIDE))
-    left = split(blocks(outer_c, -outer_s, -outer_s, -outer_c))
-    return left, right
-
-
-def spectrum(left, right, beam):
-    mine = ((iota((2 * SIDE, 2 * SIDE), 0) & (SIDE - 1)) >> 4) == beam
+    c, s = cos_sin((whole.astype(F32) + signed.astype(F32) * as_row(frac)) * (1.0 / SIDE))
+    cosines = col < SIDE // 2
+    hi, lo = split(jnp.concatenate([jnp.where(cosines, c, -s), jnp.where(cosines, -s, -c)], axis=0))
+    return jnp.concatenate([hi, hi, lo], axis=1), right
+
+
+def spectrum(left, right, column):
+    mine = ((iota((SIDE, 2 * SIDE), 0) & (SIDE // 2 - 1)) >> 4) == column
     hi, lo = [jnp.where(mine, x.astype(F32), 0.0).astype(BF16) for x in right]
-    return dot3(left[0], left[1], hi, lo)
+    return dot(left, jnp.concatenate([hi, lo, hi], axis=0))
 
 
 def side_by_side(*parts):
@@ -162,13 +158,16 @@
     lag_hbm, frac_hbm, amp_hbm, packed_hbm, ambient_hbm, pulse_hbm,
     out_ref,
     lag_ref, frac_ref, amp_ref, packed_ref, ambient_ref, pulse_ref,
-    own, gathered, echo_left, echo_right, left_tab, right_tab, twist_tab, inner_tab, outer_tab,
+    own, gathered, extra, left_tab, right_tab, twist_tab, inner_tab, outer_tab,
     ready, arrived,
-    in_sem, pulse_send, pulse_recv, hist_send, hist_recv, go_sem, near_sem,
+    in_sem, extra_send, extra_recv, pulse_send, pulse_recv, hist_send, hist_recv, go_sem, near_sem,
 ):
     me_range, me_az = lax.axis_index("range"), lax.axis_index("az")
     y, x = me_az // SIDE_AZ, lax.rem(me_az, SIDE_AZ)
     chief = GROUP - 1
+    early = me_range < HALF
+    late = jnp.logical_not(early)
+    partner = lax.rem(me_range + HALF, GROUP)
 
     def remote(src, dst, send, recv, **where):
         return pltpu.make_async_remote_copy(
@@ -201,11 +200,15 @@
     def _():
         pl.semaphore_signal(barrier, inc=1, device_id={"range": chief}, device_id_type=MESH)
 
+    @pl.when(early)
+    def _():
+        pl.semaphore_signal(barrier, inc=1, device_id={"range": partner}, device_id_type=MESH)
+
     fetches[0].wait()
     for b in range(BEAMS):
         for part in range(2):
             for q in range(8):
-                own[b, part, q : q + 1, :] = pulse_ref[b, part : part + 1, q * SIDE : (q + 1) * SIDE]
+                own[b % 2, b // 2, part, q : q + 1, :] = pulse_ref[b, part : part + 1, q * SIDE : (q + 1) * SIDE]
     for fetch in fetches[1:]:
         fetch.wait()
     first = me_range * BEAMS
@@ -216,26 +219,38 @@
         pltpu.roll(v, lax.rem(2 * SIDE + BEAMS * i - first, SIDE), 1)
         for i, v in enumerate((delay, frac_ref[0], amp))
     ]
-    lane = iota((SLOTS, SIDE), 1)
+    lane = iota((SLOTS, SIDE), 1) & (SIDE // 2 - 1)
     echo = jnp.where(lane < BEAMS, delay, jnp.where(lane < 2 * BEAMS, frac, amp))
-    for b in range(0, BEAMS, 2):
-        own[b, 2] = echo
-
-    pl.semaphore_wait(barrier, GROUP - 1 + jnp.where(me_range == chief, GROUP - 1, 0))
+    for b in range(SIDE_AZ):
+        own[0, b, 2] = echo
+
+    pl.semaphore_wait(
+        barrier,
+        GROUP - 1 + jnp.where(early, 0, 1) + jnp.where(me_range == chief, GROUP - 1, 0),
+    )
+    parts = pl.ds(0, 2)
+    extra_copy = remote(own.at[1, :, parts], extra, extra_send, extra_recv, range=partner)
+
+    @pl.when(late)
+    def _():
+        extra_copy.start()
 
     def share(k, carry):
         peer = lax.rem(me_az + k, GROUP)
-        beam = 2 * lax.rem(peer, SIDE_AZ)
-        remote(own.at[beam], gathered.at[0, me_az], pulse_send, pulse_recv.at[0], az=peer).start()
+        mine = own.at[0, lax.rem(peer, SIDE_AZ)]
+        remote(mine, gathered.at[0, me_az], pulse_send, pulse_recv.at[0], az=peer).start()
         return carry
 
     def share_next(k, carry):
         peer = lax.rem(me_az + k, GROUP)
-        beam = 2 * lax.rem(peer, SIDE_AZ) + 1
-        parts = pl.ds(0, 2)
-        remote(
-            own.at[beam, parts], gathered.at[1, me_az, parts], pulse_send, pulse_recv.at[1], az=peer
-        ).start()
+        mine = own.at[1, lax.rem(peer, SIDE_AZ), parts]
+        remote(mine, gathered.at[1, me_az, parts], pulse_send, pulse_recv.at[1], az=peer).start()
+        return carry
+
+    def share_extra(k, carry):
+        peer = lax.rem(me_az + k, GROUP)
+        mine = extra.at[lax.rem(peer, SIDE_AZ)]
+        remote(mine, gathered.at[2, me_az, parts], pulse_send, pulse_recv.at[2], az=peer).start()
         return carry
 
     lax.fori_loop(1, GROUP, share, 0)
@@ -249,8 +264,8 @@
 
         lax.fori_loop(0, GROUP - 1, tell, 0)
 
-    gathered[0, me_az] = own[2 * x]
-    gathered[1, me_az] = own[2 * x + 1]
+    gathered[0, me_az] = own[0, x]
+    gathered[1, me_az] = own[1, x]
 
     left, right, twist = dft_tables()
     left_tab[...] = side_by_side(left[0], left[0], left[1])
@@ -269,16 +284,16 @@
 
     some = gathered.at[0, pl.ds(0, GROUP - 1)]
     remote(some, some, pulse_send, pulse_recv.at[0], az=me_az).wait_recv()
-    rows = []
-    for i in range(SIDE_AZ):
-        rows.append(gathered[0, y * SIDE_AZ + i, 2])
-        rows.append(gathered[0, lax.rem(y * SIDE_AZ + i + GROUP - 1, GROUP), 2])
-    rows = stacked(*(rows * 2))
-    place = 2 * x + (iota((SIDE, SIDE), 0) >> 6)
-    delay, frac, amp = [as_column(rows, place + BEAMS * i) for i in range(3)]
-    far = (iota((SIDE, 1), 0) & SLOTS) != 0
-    amp = jnp.where(far == (delay >= TIME_SLOTS), amp, 0.0)
-    (echo_left[0], echo_left[1]), (echo_right[0], echo_right[1]) = phase_tables(delay, frac, amp)
+    def phases(j):
+        rows = []
+        for i in range(SIDE_AZ):
+            rows.append(gathered[0, y * SIDE_AZ + i, 2])
+            rows.append(gathered[0, lax.rem(y * SIDE_AZ + i + GROUP - 1, GROUP), 2])
+        rows = stacked(*rows)
+        place = 2 * x + jnp.where(j == 0, 0, 1) + jnp.where(j == 2, SIDE // 2, 0)
+        delay, frac, amp = [as_column(rows, place + BEAMS * i) for i in range(3)]
+        far = (iota(delay.shape, 0) & SLOTS) != 0
+        return phase_tables(delay, frac, jnp.where(far == (delay >= TIME_SLOTS), amp, 0.0))
 
     def tiles_of(row, count):
         return pl.ds(pl.multiple_of(row * 8, 8), count * 8)
@@ -286,12 +301,16 @@
     def tiles(ref, row, count):
         return ref.at[tiles_of(row, count)]
 
+    def beam_of(j):
+        block = jnp.where(j == 2, partner, me_range)
+        return block * BEAMS + 2 * x + jnp.where(j == 0, 0, 1)
+
     def send_tile(j, i, peer):
         @pl.when((peer != me_range) | (i != x))
         def _():
             remote(
                 tiles(ready, (j * SIDE_AZ + i) * GROUP + peer, 1),
-                tiles(arrived, me_range * BEAMS + 2 * x + j, 1),
+                tiles(arrived, beam_of(j), 1),
                 hist_send, hist_recv, range=peer, az=y * SIDE_AZ + i,
             ).start()
 
@@ -305,15 +324,15 @@
         lax.fori_loop(0, SIDE_AZ, column, 0)
 
     def work(j, carry):
-        @pl.when(j == 1)
-        def _():
-            some = gathered.at[1, pl.ds(0, GROUP - 1), pl.ds(0, 2)]
-            remote(some, some, pulse_send, pulse_recv.at[1], az=me_az).wait_recv()
-
-        e_left, e_right = (echo_left[0], echo_left[1]), (echo_right[0], echo_right[1])
-        specs = [spectrum(e_left, e_right, j * SIDE_AZ + i) for i in range(SIDE_AZ)]
+        @pl.when(j > 0)
+        def _():
+            some = gathered.at[1, pl.ds(0, GROUP - 1), parts]
+            remote(some, some, pulse_send, pulse_recv.at[j], az=me_az).wait_recv()
+
+        e_left, e_right = phases(j)
+        specs = [spectrum(e_left, e_right, i) for i in range(SIDE_AZ)]
         pulse = [gathered[j, :, part].reshape(SIDE, SIDE) for part in range(2)]
-        mine = iota((1, SIDE), 1) == first + 2 * x + j
+        mine = iota((1, SIDE), 1) == beam_of(j)
         ambient = jnp.sum(jnp.where(mine, ambient_ref[...], 0.0), axis=1, keepdims=True)
         hist = group_histogram(
             specs, [pulse] * SIDE_AZ, [ambient] * SIDE_AZ, left_tab[...], right_tab[...],
@@ -325,30 +344,64 @@
         def _():
             pl.semaphore_wait(near_sem, SIDE_AZ - 1)
 
-        send_tiles(j, EARLY_ORDER)
+        @pl.when(early | (j == 0))
+        def _():
+            send_tiles(j, EARLY_ORDER)
+
+        @pl.when(early & (j == 0))
+        def _():
+            extra_copy.wait_recv()
+            lax.fori_loop(1, GROUP, share_extra, 0)
+            gathered[2, me_az, :2] = extra[x]
+
+        @pl.when(j == 1)
+        def _():
+            send_tiles(0, LATE_ORDER)
+            send_tiles(1, LATE_ORDER)
+
         return carry
 
-    lax.fori_loop(0, 2, work, 0)
-    send_tiles(0, LATE_ORDER)
-    send_tiles(1, LATE_ORDER)
-    for j in range(2):
-        arrived[tiles_of(me_range * BEAMS + 2 * x + j, 1), :] = ready[
-            tiles_of((j * SIDE_AZ + x) * GROUP + me_range, 1), :
-        ]
-
-    some = tiles(arrived, 0, GROUP * BEAMS - 2)
-    done = remote(some, some, hist_send, hist_recv, az=me_az)
-    done.wait_recv()
+    lax.fori_loop(0, jnp.where(early, 3, 2), work, 0)
+
+    def keep(j):
+        arrived[tiles_of(beam_of(j), 1), :] = ready[tiles_of((j * SIDE_AZ + x) * GROUP + me_range, 1), :]
+
+    def settled(ref, send, recv, count):
+        some = tiles(ref, 0, count)
+        return remote(some, some, send, recv, az=me_az)
+
+    keep(0)
+    keep(1)
+
+    @pl.when(early)
+    def _():
+        keep(2)
+        settled(arrived, hist_send, hist_recv, GROUP * BEAMS - 3).wait_recv()
+
+    @pl.when(late)
+    def _():
+        settled(arrived, hist_send, hist_recv, GROUP * BEAMS - 2).wait_recv()
+
     for g in range(GROUP):
         for s in range(8):
             out_ref[0, g * 8 : (g + 1) * 8, s * SIDE : (s + 1) * SIDE] = arrived[
                 pl.ds(g * 64 + s, 8, stride=8), :
             ]
-    done.wait_send()
     some = gathered.at[0, pl.ds(0, GROUP - 1)]
     remote(some, some, pulse_send, pulse_recv.at[0], az=me_az).wait_send()
-    some = gathered.at[1, pl.ds(0, GROUP - 1), pl.ds(0, 2)]
+    some = gathered.at[1, pl.ds(0, GROUP - 1), parts]
     remote(some, some, pulse_send, pulse_recv.at[1], az=me_az).wait_send()
+    tiles_all, tiles_half = SIDE_AZ * GROUP - 1, SIDE_AZ * HALF - 1
+
+    @pl.when(early)
+    def _():
+        remote(some, some, pulse_send, pulse_recv.at[1], az=me_az).wait_send()
+        settled(ready, hist_send, hist_recv, 2 * tiles_all + tiles_half).wait_send()
+
+    @pl.when(late)
+    def _():
+        extra_copy.wait_send()
+        settled(ready, hist_send, hist_recv, tiles_all + tiles_half).wait_send()
 
 
 def per_device(lag, frac, amp, offset, count, ambient, pulse):
@@ -367,18 +420,17 @@
             pltpu.VMEM((1, 1), jnp.int32),
             pltpu.VMEM((1, SIDE), F32),
             pltpu.VMEM((BEAMS, 2, TIME_SLOTS // GROUP), F32),
-            pltpu.VMEM((BEAMS, 3, 8, SIDE), F32),
-            pltpu.VMEM((2, GROUP, 3, 8, SIDE), F32),
-            pltpu.VMEM((2, 2 * SIDE, 2 * SIDE), BF16),
-            pltpu.VMEM((2, 2 * SIDE, 2 * SIDE), BF16),
+            pltpu.VMEM((2, SIDE_AZ, 3, 8, SIDE), F32),
+            pltpu.VMEM((3, GROUP, 3, 8, SIDE), F32),
+            pltpu.VMEM((SIDE_AZ, 2, 8, SIDE), F32),
             pltpu.VMEM((2 * SIDE, 6 * SIDE), BF16),
             pltpu.VMEM((6 * SIDE, 2 * SIDE), BF16),
             pltpu.VMEM((2, SIDE, SIDE), F32),
             pltpu.VMEM((2 * SIDE, 2 * SIDE), BF16),
             pltpu.VMEM((SIDE, 2 * SIDE), BF16),
+            pltpu.VMEM((3 * SIDE_AZ * SIDE, SIDE), F32),
             pltpu.VMEM((GROUP * BEAMS * 8, SIDE), F32),
-            pltpu.VMEM((GROUP * BEAMS * 8, SIDE), F32),
-            dma((6,)), dma, dma((2,)), dma, dma,
+            dma((6,)), dma, dma, dma, dma((3,)), dma, dma,
             pltpu.SemaphoreType.REGULAR, pltpu.SemaphoreType.REGULAR,
         ],
         compiler_params=pltpu.CompilerParams(

time: 35.2 us -> 35.9 us (1.020)
  Pallas kernels: 31.3 us -> 32.1 us
    pallas_call x1, Pallas kernels: 31.3 us -> 32.1 us  [per_device(): pl.pallas_call(kernel, out_shape=jax.ShapeDtypeStruct((1, GROUP * BEAMS,...]
where the time goes in v4:
time: 35.9 us; the launch traced here: 35.8 us
  Pallas kernels  32.1 us (89%)
  local copies, waits for them, and re-layouts  2.32 us (6%)
  between operations  1.34 us (4%)
    pallas_call x1, Pallas kernels, per_device(): pl.pallas_call(kernel, out_shape=jax.ShapeDtypeStruct((1, GROUP * BEAMS,...  32.1 us
    unnamed x11, local copies, waits for them, and re-layouts  2.32 us

profile of v4, /device:TPU:1, one launch (start us, length us, event | category | flops | bytes accessed | tf_op | source)
XLA Modules:
  0.0 35.8 jit_solution(2134374982411855422)
XLA Ops:
  1.3 0.0 copy-start.3
  1.3 0.0 copy-start.2
  1.3 0.0 copy-start.1
  1.3 0.0 copy-start.4
  1.3 0.6 %copy-done.3 = f32[1,128,8]{1,2,0:T(8,128)S(1)} copy-done((f32[1,128,8]{1,2,0:T(8,128)S(1)}, f32[1,128,8]{1,2,0:T(8,128)}, u32[]{:S(2)}) %copy-start.3) | copy-done | bytes 4120
  2.0 0.0 copy-done.2
  2.0 0.0 copy-done.1
  2.0 0.0 copy-done.4
  2.0 0.0 copy-start
  2.0 0.8 %copy-done = f32[8,2,1024]{2,1,0:T(2,128)S(1)} copy-done((f32[8,2,1024]{2,1,0:T(2,128)S(1)}, f32[8,2,1024]{2,1,0:T(2,128)}, u32[]{:S(2)}) %copy-start) | copy-done | bytes 65560
  2.9 32.1 %shard_map.73 = f32[1,128,1024]{2,1,0:T(8,128)S(1)} custom-call(s32[1,8,128]{2,1,0:T(8,128)S(1)} %bitcast.5, f32[1,8,128]{2,1,0:T(8,128)S(1)} %bitcast.6, f32[1,8,128]{2,1,0:T(8,128)S(1)} %bitcast.7, s32[1,1]{1,0:T(1,128)} %bitcast.3.packed_hbm, f32[1,128]{1,0:T(1,128)S(1)} %bitcast.8, f32[8,2,1024]{2,1,0:T(2,128)S(1)} %copy-done), custom_call_target="tpu_custom_call" | custom-call | tf_op jit(solution)/shard_map/pallas_call | solution.py:411
  35.0 0.8 %copy.11 = f32[1,128,1024]{2,1,0:T(8,128)} copy(f32[1,128,1024]{2,1,0:T(8,128)S(1)} %shard_map.73) | data formatting | bytes 1048576
Async XLA Ops:
  1.3 0.7 %copy-start.3 = (f32[1,128,8]{1,2,0:T(8,128)S(1)}, f32[1,128,8]{1,2,0:T(8,128)}, u32[]{:S(2)}) copy-start(f32[1,128,8]{1,2,0:T(8,128)} %param.9) | copy-start | bytes 12292
  1.3 0.7 %copy-start.2 = (f32[1,128,8]{1,2,0:T(8,128)S(1)}, f32[1,128,8]{1,2,0:T(8,128)}, u32[]{:S(2)}) copy-start(f32[1,128,8]{1,2,0:T(8,128)} %param.8) | copy-start | bytes 12292
  1.3 0.7 %copy-start.1 = (s32[1,128,8]{1,2,0:T(8,128)S(1)}, s32[1,128,8]{1,2,0:T(8,128)}, u32[]{:S(2)}) copy-start(s32[1,128,8]{1,2,0:T(8,128)} %param.7) | copy-start | bytes 12292
  1.3 0.7 %copy-start.4 = (f32[128]{0:T(128)S(1)}, f32[128]{0:T(128)}, u32[]{:S(2)}) copy-start(f32[128]{0:T(128)} %param.12) | copy-start | bytes 1540
  2.0 0.8 %copy-start = (f32[8,2,1024]{2,1,0:T(2,128)S(1)}, f32[8,2,1024]{2,1,0:T(2,128)}, u32[]{:S(2)}) copy-start(f32[8,2,1024]{2,1,0:T(2,128)} %pulse_hbm.1) | copy-start | bytes 196612

commit v5 on v4

--- a/solution.py
+++ b/solution.py
@@ -13,8 +13,6 @@
 SLOTS = 8
 GROUP = 16
 HALF = 8
-EARLY_ORDER = (1, 0, 7, 6, 3, 2, 5, 4)
-LATE_ORDER = (8, 9, 14, 15, 10, 11, 12, 13)
 SIDE_AZ = 4
 MESH = pl.DeviceIdType.MESH
 F32 = jnp.float32
@@ -158,12 +156,15 @@
     lag_hbm, frac_hbm, amp_hbm, packed_hbm, ambient_hbm, pulse_hbm,
     out_ref,
     lag_ref, frac_ref, amp_ref, packed_ref, ambient_ref, pulse_ref,
-    own, gathered, extra, left_tab, right_tab, twist_tab, inner_tab, outer_tab,
+    own, echoes, gathered, extra, left_tab, right_tab, twist_tab, inner_tab, outer_tab,
     ready, arrived,
-    in_sem, extra_send, extra_recv, pulse_send, pulse_recv, hist_send, hist_recv, go_sem, near_sem,
+    in_sem, echo_send, echo_recv, extra_send, extra_recv, pulse_send, pulse_recv, hist_send, hist_recv, go_sem, near_sem,
 ):
     me_range, me_az = lax.axis_index("range"), lax.axis_index("az")
     y, x = me_az // SIDE_AZ, lax.rem(me_az, SIDE_AZ)
+    odd = lax.rem(y, 2)
+    row_pair = y - odd
+    pair_place = lax.rem(me_az, HALF)
     chief = GROUP - 1
     early = me_range < HALF
     late = jnp.logical_not(early)
@@ -208,7 +209,7 @@
     for b in range(BEAMS):
         for part in range(2):
             for q in range(8):
-                own[b % 2, b // 2, part, q : q + 1, :] = pulse_ref[b, part : part + 1, q * SIDE : (q + 1) * SIDE]
+                own[b, part, q : q + 1, :] = pulse_ref[b, part : part + 1, q * SIDE : (q + 1) * SIDE]
     for fetch in fetches[1:]:
         fetch.wait()
     first = me_range * BEAMS
@@ -220,41 +221,49 @@
         for i, v in enumerate((delay, frac_ref[0], amp))
     ]
     lane = iota((SLOTS, SIDE), 1) & (SIDE // 2 - 1)
-    echo = jnp.where(lane < BEAMS, delay, jnp.where(lane < 2 * BEAMS, frac, amp))
-    for b in range(SIDE_AZ):
-        own[0, b, 2] = echo
+    echoes[me_az] = jnp.where(lane < BEAMS, delay, jnp.where(lane < 2 * BEAMS, frac, amp))
 
     pl.semaphore_wait(
         barrier,
         GROUP - 1 + jnp.where(early, 0, 1) + jnp.where(me_range == chief, GROUP - 1, 0),
     )
-    parts = pl.ds(0, 2)
-    extra_copy = remote(own.at[1, :, parts], extra, extra_send, extra_recv, range=partner)
+    extra_copy = remote(own, extra, extra_send, extra_recv, range=partner)
 
     @pl.when(late)
     def _():
         extra_copy.start()
+
+    def share_echo(peer):
+        mine = echoes.at[me_az]
+        remote(mine, mine, echo_send, echo_recv, az=peer).start()
+
+    def share_near(k, carry):
+        share_echo(row_pair * SIDE_AZ + lax.rem(pair_place + k, HALF))
+        return carry
+
+    lax.fori_loop(1, HALF, share_near, 0)
+
+    @pl.when(pair_place == HALF - 1)
+    def _():
+        def share_far(k, carry):
+            share_echo(lax.rem(me_az + 1 + k, GROUP))
+            return carry
+
+        lax.fori_loop(0, HALF, share_far, 0)
 
     def share(k, carry):
         peer = lax.rem(me_az + k, GROUP)
-        mine = own.at[0, lax.rem(peer, SIDE_AZ)]
-        remote(mine, gathered.at[0, me_az], pulse_send, pulse_recv.at[0], az=peer).start()
-        return carry
-
-    def share_next(k, carry):
-        peer = lax.rem(me_az + k, GROUP)
-        mine = own.at[1, lax.rem(peer, SIDE_AZ), parts]
-        remote(mine, gathered.at[1, me_az, parts], pulse_send, pulse_recv.at[1], az=peer).start()
+        beam = lax.rem(peer, HALF)
+        remote(own.at[beam], gathered.at[0, me_az], pulse_send, pulse_recv.at[0], az=peer).start()
         return carry
 
     def share_extra(k, carry):
         peer = lax.rem(me_az + k, GROUP)
-        mine = extra.at[lax.rem(peer, SIDE_AZ)]
-        remote(mine, gathered.at[2, me_az, parts], pulse_send, pulse_recv.at[2], az=peer).start()
+        beam = lax.rem(peer + SIDE_AZ, HALF)
+        remote(extra.at[beam], gathered.at[1, me_az], pulse_send, pulse_recv.at[1], az=peer).start()
         return carry
 
     lax.fori_loop(1, GROUP, share, 0)
-    lax.fori_loop(1, GROUP, share_next, 0)
 
     @pl.when(me_range == chief)
     def _():
@@ -264,8 +273,7 @@
 
         lax.fori_loop(0, GROUP - 1, tell, 0)
 
-    gathered[0, me_az] = own[0, x]
-    gathered[1, me_az] = own[1, x]
+    gathered[0, me_az] = own[pair_place]
 
     left, right, twist = dft_tables()
     left_tab[...] = side_by_side(left[0], left[0], left[1])
@@ -273,24 +281,36 @@
     twist_tab[0], twist_tab[1] = twist
     inner_tab[...], outer_tab[...] = prefix_tables()
 
-    @pl.when(me_range != chief)
-    def _():
-        pl.semaphore_wait(go_sem, 1)
-
-    for k in range(1, SIDE_AZ):
-        pl.semaphore_signal(
-            near_sem, inc=1, device_id={"az": y * SIDE_AZ + lax.rem(x + k, SIDE_AZ)}, device_id_type=MESH
-        )
-
-    some = gathered.at[0, pl.ds(0, GROUP - 1)]
-    remote(some, some, pulse_send, pulse_recv.at[0], az=me_az).wait_recv()
+    def pass_on():
+        @pl.when(me_range != chief)
+        def _():
+            pl.semaphore_wait(go_sem, 1)
+
+        for k in range(1, HALF):
+            peer = row_pair * SIDE_AZ + lax.rem(pair_place + k, HALF)
+            pl.semaphore_signal(near_sem, inc=1, device_id={"az": peer}, device_id_type=MESH)
+
+    pl.when(late)(pass_on)
+
+    some_echoes = echoes.at[pl.ds(0, HALF)]
+    remote(some_echoes, some_echoes, echo_send, echo_recv, az=me_az).wait_recv()
+    fifteen = gathered.at[0, pl.ds(0, GROUP - 1)]
+    remote(fifteen, fifteen, pulse_send, pulse_recv.at[0], az=me_az).wait_recv()
+
+    def row_of(j):
+        return y + jnp.where(j == 1, 1 - 2 * odd, 0)
+
+    def beam_of(j):
+        return x + SIDE_AZ * jnp.where(j == 2, 1 - odd, odd)
+
     def phases(j):
         rows = []
         for i in range(SIDE_AZ):
-            rows.append(gathered[0, y * SIDE_AZ + i, 2])
-            rows.append(gathered[0, lax.rem(y * SIDE_AZ + i + GROUP - 1, GROUP), 2])
+            column = row_of(j) * SIDE_AZ + i
+            rows.append(echoes[column])
+            rows.append(echoes[lax.rem(column + GROUP - 1, GROUP)])
         rows = stacked(*rows)
-        place = 2 * x + jnp.where(j == 0, 0, 1) + jnp.where(j == 2, SIDE // 2, 0)
+        place = beam_of(j) + jnp.where(j == 2, SIDE // 2, 0)
         delay, frac, amp = [as_column(rows, place + BEAMS * i) for i in range(3)]
         far = (iota(delay.shape, 0) & SLOTS) != 0
         return phase_tables(delay, frac, jnp.where(far == (delay >= TIME_SLOTS), amp, 0.0))
@@ -301,38 +321,43 @@
     def tiles(ref, row, count):
         return ref.at[tiles_of(row, count)]
 
-    def beam_of(j):
-        block = jnp.where(j == 2, partner, me_range)
-        return block * BEAMS + 2 * x + jnp.where(j == 0, 0, 1)
+    def whole_beam(j):
+        return jnp.where(j == 2, partner, me_range) * BEAMS + beam_of(j)
 
     def send_tile(j, i, peer):
-        @pl.when((peer != me_range) | (i != x))
+        column = row_of(j) * SIDE_AZ + i
+
+        @pl.when((peer != me_range) | (column != me_az))
         def _():
             remote(
-                tiles(ready, (j * SIDE_AZ + i) * GROUP + peer, 1),
-                tiles(arrived, beam_of(j), 1),
-                hist_send, hist_recv, range=peer, az=y * SIDE_AZ + i,
+                tiles(ready, (j * SIDE_AZ + i) * GROUP + peer, 1), tiles(arrived, whole_beam(j), 1),
+                hist_send, hist_recv, range=peer, az=column,
             ).start()
 
-    def send_tiles(j, order):
-        def column(k, carry):
-            i = lax.rem(x + k, SIDE_AZ)
-            for peer in order:
-                send_tile(j, i, peer)
-            return carry
-
-        lax.fori_loop(0, SIDE_AZ, column, 0)
+    def send_tiles(j, half):
+        away = half != me_range // HALF
+        high, low = me_range // 4 - 2 * (me_range // HALF), lax.rem(me_range // 2, 2)
+        for turn in range(4):
+            t1, t0 = jnp.where(away, turn // 2, 1 - turn // 2), jnp.where(away, turn % 2, 1 - turn % 2)
+            plane = 2 * (high + t1 - 2 * high * t1) + low + t0 - 2 * low * t0
+
+            def column(k, carry):
+                for c in (1, 0):
+                    send_tile(j, lax.rem(x + k, SIDE_AZ), half * HALF + 2 * plane + c)
+                return carry
+
+            lax.fori_loop(0, SIDE_AZ, column, 0)
 
     def work(j, carry):
-        @pl.when(j > 0)
-        def _():
-            some = gathered.at[1, pl.ds(0, GROUP - 1), parts]
-            remote(some, some, pulse_send, pulse_recv.at[j], az=me_az).wait_recv()
+        @pl.when(j == 2)
+        def _():
+            remote(fifteen, fifteen, pulse_send, pulse_recv.at[1], az=me_az).wait_recv()
 
         e_left, e_right = phases(j)
         specs = [spectrum(e_left, e_right, i) for i in range(SIDE_AZ)]
-        pulse = [gathered[j, :, part].reshape(SIDE, SIDE) for part in range(2)]
-        mine = iota((1, SIDE), 1) == beam_of(j)
+        source = jnp.where(j == 2, 1, 0)
+        pulse = [gathered[source, :, part].reshape(SIDE, SIDE) for part in range(2)]
+        mine = iota((1, SIDE), 1) == whole_beam(j)
         ambient = jnp.sum(jnp.where(mine, ambient_ref[...], 0.0), axis=1, keepdims=True)
         hist = group_histogram(
             specs, [pulse] * SIDE_AZ, [ambient] * SIDE_AZ, left_tab[...], right_tab[...],
@@ -340,68 +365,77 @@
         )
         ready[tiles_of(j * SIDE_AZ * GROUP, SIDE_AZ * GROUP), :] = hist
 
-        @pl.when(j == 0)
-        def _():
-            pl.semaphore_wait(near_sem, SIDE_AZ - 1)
-
-        @pl.when(early | (j == 0))
-        def _():
-            send_tiles(j, EARLY_ORDER)
-
         @pl.when(early & (j == 0))
         def _():
             extra_copy.wait_recv()
             lax.fori_loop(1, GROUP, share_extra, 0)
-            gathered[2, me_az, :2] = extra[x]
-
-        @pl.when(j == 1)
-        def _():
-            send_tiles(0, LATE_ORDER)
-            send_tiles(1, LATE_ORDER)
+            gathered[1, me_az] = extra[beam_of(2)]
+
+        @pl.when(j == 0)
+        def _():
+            pl.when(early)(pass_on)
+            pl.semaphore_wait(near_sem, HALF - 1)
+
+        @pl.when(early | (j == 0))
+        def _():
+            send_tiles(j, 0)
+
+        @pl.when(j == 0)
+        def _():
+            send_tiles(0, 1)
+
+        @pl.when((j == jnp.where(early, 2, 1)))
+        def _():
+            send_tiles(1, 1)
 
         return carry
 
     lax.fori_loop(0, jnp.where(early, 3, 2), work, 0)
 
     def keep(j):
-        arrived[tiles_of(beam_of(j), 1), :] = ready[tiles_of((j * SIDE_AZ + x) * GROUP + me_range, 1), :]
+        arrived[tiles_of(whole_beam(j), 1), :] = ready[
+            tiles_of((j * SIDE_AZ + x) * GROUP + me_range, 1), :
+        ]
 
     def settled(ref, send, recv, count):
         some = tiles(ref, 0, count)
         return remote(some, some, send, recv, az=me_az)
 
     keep(0)
-    keep(1)
 
     @pl.when(early)
     def _():
         keep(2)
-        settled(arrived, hist_send, hist_recv, GROUP * BEAMS - 3).wait_recv()
+        settled(arrived, hist_send, hist_recv, GROUP * BEAMS - 2).wait_recv()
 
     @pl.when(late)
     def _():
-        settled(arrived, hist_send, hist_recv, GROUP * BEAMS - 2).wait_recv()
+        settled(arrived, hist_send, hist_recv, GROUP * BEAMS - 1).wait_recv()
 
     for g in range(GROUP):
         for s in range(8):
             out_ref[0, g * 8 : (g + 1) * 8, s * SIDE : (s + 1) * SIDE] = arrived[
                 pl.ds(g * 64 + s, 8, stride=8), :
             ]
-    some = gathered.at[0, pl.ds(0, GROUP - 1)]
-    remote(some, some, pulse_send, pulse_recv.at[0], az=me_az).wait_send()
-    some = gathered.at[1, pl.ds(0, GROUP - 1), parts]
-    remote(some, some, pulse_send, pulse_recv.at[1], az=me_az).wait_send()
-    tiles_all, tiles_half = SIDE_AZ * GROUP - 1, SIDE_AZ * HALF - 1
+    remote(fifteen, fifteen, pulse_send, pulse_recv.at[0], az=me_az).wait_send()
+    seven = echoes.at[pl.ds(0, HALF - 1)]
+    remote(seven, seven, echo_send, echo_recv, az=me_az).wait_send()
+
+    @pl.when(pair_place == HALF - 1)
+    def _():
+        remote(some_echoes, some_echoes, echo_send, echo_recv, az=me_az).wait_send()
+
+    tiles_all, tiles_half = SIDE_AZ * GROUP, SIDE_AZ * HALF
 
     @pl.when(early)
     def _():
-        remote(some, some, pulse_send, pulse_recv.at[1], az=me_az).wait_send()
-        settled(ready, hist_send, hist_recv, 2 * tiles_all + tiles_half).wait_send()
+        remote(fifteen, fifteen, pulse_send, pulse_recv.at[1], az=me_az).wait_send()
+        settled(ready, hist_send, hist_recv, 2 * tiles_all + tiles_half - 2).wait_send()
 
     @pl.when(late)
     def _():
         extra_copy.wait_send()
-        settled(ready, hist_send, hist_recv, tiles_all + tiles_half).wait_send()
+        settled(ready, hist_send, hist_recv, tiles_all + tiles_half - 1).wait_send()
 
 
 def per_device(lag, frac, amp, offset, count, ambient, pulse):
@@ -420,9 +454,10 @@
             pltpu.VMEM((1, 1), jnp.int32),
             pltpu.VMEM((1, SIDE), F32),
             pltpu.VMEM((BEAMS, 2, TIME_SLOTS // GROUP), F32),
-            pltpu.VMEM((2, SIDE_AZ, 3, 8, SIDE), F32),
-            pltpu.VMEM((3, GROUP, 3, 8, SIDE), F32),
-            pltpu.VMEM((SIDE_AZ, 2, 8, SIDE), F32),
+            pltpu.VMEM((BEAMS, 2, 8, SIDE), F32),
+            pltpu.VMEM((GROUP, SLOTS, SIDE), F32),
+            pltpu.VMEM((2, GROUP, 2, 8, SIDE), F32),
+            pltpu.VMEM((BEAMS, 2, 8, SIDE), F32),
             pltpu.VMEM((2 * SIDE, 6 * SIDE), BF16),
             pltpu.VMEM((6 * SIDE, 2 * SIDE), BF16),
             pltpu.VMEM((2, SIDE, SIDE), F32),
@@ -430,7 +465,7 @@
             pltpu.VMEM((SIDE, 2 * SIDE), BF16),
             pltpu.VMEM((3 * SIDE_AZ * SIDE, SIDE), F32),
             pltpu.VMEM((GROUP * BEAMS * 8, SIDE), F32),
-            dma((6,)), dma, dma, dma, dma((3,)), dma, dma,
+            dma((6,)), dma, dma, dma, dma, dma, dma((2,)), dma, dma,
             pltpu.SemaphoreType.REGULAR, pltpu.SemaphoreType.REGULAR,
         ],
         compiler_params=pltpu.CompilerParams(

time: 35.9 us -> 36.5 us (1.017)
  Pallas kernels: 32.1 us -> 32.6 us
    pallas_call x1, Pallas kernels: 32.1 us -> 32.6 us  [per_device(): pl.pallas_call(kernel, out_shape=jax.ShapeDtypeStruct((1, GROUP * BEAMS,...]
where the time goes in v5:
time: 36.5 us; the launch traced here: 36.3 us
  Pallas kernels  32.6 us (89%)
  local copies, waits for them, and re-layouts  2.32 us (6%)
  between operations  1.34 us (4%)
    pallas_call x1, Pallas kernels, per_device(): pl.pallas_call(kernel, out_shape=jax.ShapeDtypeStruct((1, GROUP * BEAMS,...  32.6 us
    unnamed x11, local copies, waits for them, and re-layouts  2.32 us

profile of v5, /device:TPU:1, one launch (start us, length us, event | category | flops | bytes accessed | tf_op | source)
XLA Modules:
  0.0 36.3 jit_solution(10811384608776107108)
XLA Ops:
  1.3 0.0 copy-start.3
  1.3 0.0 copy-start.2
  1.3 0.0 copy-start.1
  1.3 0.0 copy-start.4
  1.3 0.6 %copy-done.3 = f32[1,128,8]{1,2,0:T(8,128)S(1)} copy-done((f32[1,128,8]{1,2,0:T(8,128)S(1)}, f32[1,128,8]{1,2,0:T(8,128)}, u32[]{:S(2)}) %copy-start.3) | copy-done | bytes 4120
  2.0 0.0 copy-done.2
  2.0 0.0 copy-done.1
  2.0 0.0 copy-done.4
  2.0 0.0 copy-start
  2.0 0.8 %copy-done = f32[8,2,1024]{2,1,0:T(2,128)S(1)} copy-done((f32[8,2,1024]{2,1,0:T(2,128)S(1)}, f32[8,2,1024]{2,1,0:T(2,128)}, u32[]{:S(2)}) %copy-start) | copy-done | bytes 65560
  2.9 32.6 %shard_map.73 = f32[1,128,1024]{2,1,0:T(8,128)S(1)} custom-call(s32[1,8,128]{2,1,0:T(8,128)S(1)} %bitcast.5, f32[1,8,128]{2,1,0:T(8,128)S(1)} %bitcast.6, f32[1,8,128]{2,1,0:T(8,128)S(1)} %bitcast.7, s32[1,1]{1,0:T(1,128)} %bitcast.3.packed_hbm, f32[1,128]{1,0:T(1,128)S(1)} %bitcast.8, f32[8,2,1024]{2,1,0:T(2,128)S(1)} %copy-done), custom_call_target="tpu_custom_call" | custom-call | tf_op jit(solution)/shard_map/pallas_call | solution.py:445
  35.5 0.8 %copy.11 = f32[1,128,1024]{2,1,0:T(8,128)} copy(f32[1,128,1024]{2,1,0:T(8,128)S(1)} %shard_map.73) | data formatting | bytes 1048576
Async XLA Ops:
  1.3 0.7 %copy-start.3 = (f32[1,128,8]{1,2,0:T(8,128)S(1)}, f32[1,128,8]{1,2,0:T(8,128)}, u32[]{:S(2)}) copy-start(f32[1,128,8]{1,2,0:T(8,128)} %param.9) | copy-start | bytes 12292
  1.3 0.7 %copy-start.2 = (f32[1,128,8]{1,2,0:T(8,128)S(1)}, f32[1,128,8]{1,2,0:T(8,128)}, u32[]{:S(2)}) copy-start(f32[1,128,8]{1,2,0:T(8,128)} %param.8) | copy-start | bytes 12292
  1.3 0.7 %copy-start.1 = (s32[1,128,8]{1,2,0:T(8,128)S(1)}, s32[1,128,8]{1,2,0:T(8,128)}, u32[]{:S(2)}) copy-start(s32[1,128,8]{1,2,0:T(8,128)} %param.7) | copy-start | bytes 12292
  1.3 0.7 %copy-start.4 = (f32[128]{0:T(128)S(1)}, f32[128]{0:T(128)}, u32[]{:S(2)}) copy-start(f32[128]{0:T(128)} %param.12) | copy-start | bytes 1540
  2.0 0.8 %copy-start = (f32[8,2,1024]{2,1,0:T(2,128)S(1)}, f32[8,2,1024]{2,1,0:T(2,128)}, u32[]{:S(2)}) copy-start(f32[8,2,1024]{2,1,0:T(2,128)} %pulse_hbm.1) | copy-start | bytes 196612

commit v6 on v5

--- a/solution.py
+++ b/solution.py
@@ -13,6 +13,8 @@
 SLOTS = 8
 GROUP = 16
 HALF = 8
+PIECES = 4
+VMEM_LIMIT = 56 * 1024 * 1024
 SIDE_AZ = 4
 MESH = pl.DeviceIdType.MESH
 F32 = jnp.float32
@@ -154,11 +156,11 @@
 
 def kernel(
     lag_hbm, frac_hbm, amp_hbm, packed_hbm, ambient_hbm, pulse_hbm,
-    out_ref,
+    arrived,
     lag_ref, frac_ref, amp_ref, packed_ref, ambient_ref, pulse_ref,
-    own, echoes, gathered, extra, left_tab, right_tab, twist_tab, inner_tab, outer_tab,
-    ready, arrived,
-    in_sem, echo_send, echo_recv, extra_send, extra_recv, pulse_send, pulse_recv, hist_send, hist_recv, go_sem, near_sem,
+    own, echoes, gathered, extra, spec, left_tab, right_tab, twist_tab, inner_tab, outer_tab,
+    ready,
+    in_sem, keep_sem, echo_send, echo_recv, extra_send, extra_recv, pulse_send, pulse_recv, hist_send, hist_recv, go_sem, near_sem,
 ):
     me_range, me_az = lax.axis_index("range"), lax.axis_index("az")
     y, x = me_az // SIDE_AZ, lax.rem(me_az, SIDE_AZ)
@@ -166,6 +168,7 @@
     row_pair = y - odd
     pair_place = lax.rem(me_az, HALF)
     chief = GROUP - 1
+    z, core = me_range // 2, lax.rem(me_range, 2)
     early = me_range < HALF
     late = jnp.logical_not(early)
     partner = lax.rem(me_range + HALF, GROUP)
@@ -228,10 +231,7 @@
         GROUP - 1 + jnp.where(early, 0, 1) + jnp.where(me_range == chief, GROUP - 1, 0),
     )
     extra_copy = remote(own, extra, extra_send, extra_recv, range=partner)
-
-    @pl.when(late)
-    def _():
-        extra_copy.start()
+    pl.when(late)(lambda: extra_copy.start())
 
     def share_echo(peer):
         mine = echoes.at[me_az]
@@ -251,19 +251,19 @@
 
         lax.fori_loop(0, HALF, share_far, 0)
 
-    def share(k, carry):
-        peer = lax.rem(me_az + k, GROUP)
+    def share_step(source, which, dy, dx):
+        peer = lax.rem(y + dy, SIDE_AZ) * SIDE_AZ + lax.rem(x + dx, SIDE_AZ)
         beam = lax.rem(peer, HALF)
-        remote(own.at[beam], gathered.at[0, me_az], pulse_send, pulse_recv.at[0], az=peer).start()
-        return carry
-
-    def share_extra(k, carry):
-        peer = lax.rem(me_az + k, GROUP)
-        beam = lax.rem(peer + SIDE_AZ, HALF)
-        remote(extra.at[beam], gathered.at[1, me_az], pulse_send, pulse_recv.at[1], az=peer).start()
-        return carry
-
-    lax.fori_loop(1, GROUP, share, 0)
+        remote(source.at[beam], gathered.at[which, me_az], pulse_send, pulse_recv.at[which], az=peer).start()
+
+    def share(source, which):
+        for dy, dx in sorted(
+            [(i // SIDE_AZ, i % SIDE_AZ) for i in range(1, GROUP)],
+            key=lambda d: -(min(d[0], SIDE_AZ - d[0]) + min(d[1], SIDE_AZ - d[1])),
+        ):
+            share_step(source, which, dy, dx)
+
+    share(own, 0)
 
     @pl.when(me_range == chief)
     def _():
@@ -281,27 +281,11 @@
     twist_tab[0], twist_tab[1] = twist
     inner_tab[...], outer_tab[...] = prefix_tables()
 
-    def pass_on():
-        @pl.when(me_range != chief)
-        def _():
-            pl.semaphore_wait(go_sem, 1)
-
-        for k in range(1, HALF):
-            peer = row_pair * SIDE_AZ + lax.rem(pair_place + k, HALF)
-            pl.semaphore_signal(near_sem, inc=1, device_id={"az": peer}, device_id_type=MESH)
-
-    pl.when(late)(pass_on)
-
     some_echoes = echoes.at[pl.ds(0, HALF)]
     remote(some_echoes, some_echoes, echo_send, echo_recv, az=me_az).wait_recv()
-    fifteen = gathered.at[0, pl.ds(0, GROUP - 1)]
-    remote(fifteen, fifteen, pulse_send, pulse_recv.at[0], az=me_az).wait_recv()
 
     def row_of(j):
-        return y + jnp.where(j == 1, 1 - 2 * odd, 0)
-
-    def beam_of(j):
-        return x + SIDE_AZ * jnp.where(j == 2, 1 - odd, odd)
+        return y + lax.rem(j, 2) * (1 - 2 * odd)
 
     def phases(j):
         rows = []
@@ -310,19 +294,41 @@
             rows.append(echoes[column])
             rows.append(echoes[lax.rem(column + GROUP - 1, GROUP)])
         rows = stacked(*rows)
-        place = beam_of(j) + jnp.where(j == 2, SIDE // 2, 0)
-        delay, frac, amp = [as_column(rows, place + BEAMS * i) for i in range(3)]
+        delay, frac, amp = [as_column(rows, pair_place + SIDE // 2 * (j // 2) + BEAMS * i) for i in range(3)]
         far = (iota(delay.shape, 0) & SLOTS) != 0
         return phase_tables(delay, frac, jnp.where(far == (delay >= TIME_SLOTS), amp, 0.0))
 
+    def prepare(j, carry):
+        e_left, e_right = phases(j)
+        for i in range(SIDE_AZ):
+            spec[j * SIDE_AZ + i] = spectrum(e_left, e_right, i)
+        return carry
+
+    lax.fori_loop(0, 2, prepare, 0)
+    @pl.when(me_range != chief)
+    def _():
+        pl.semaphore_wait(go_sem, 1)
+
+    pl.when(early)(lambda: extra_copy.start())
+    for k in range(1, HALF):
+        peer = row_pair * SIDE_AZ + lax.rem(pair_place + k, HALF)
+        pl.semaphore_signal(near_sem, inc=1, device_id={"az": peer}, device_id_type=MESH)
+
+    fifteen = gathered.at[0, pl.ds(0, GROUP - 1)]
+
+    def wait_pulses(which):
+        remote(fifteen, fifteen, pulse_send, pulse_recv.at[which], az=me_az).wait_recv()
+
+    wait_pulses(0)
+
     def tiles_of(row, count):
         return pl.ds(pl.multiple_of(row * 8, 8), count * 8)
 
     def tiles(ref, row, count):
         return ref.at[tiles_of(row, count)]
 
-    def whole_beam(j):
-        return jnp.where(j == 2, partner, me_range) * BEAMS + beam_of(j)
+    def beam_of(j):
+        return (me_range + j // 2 * (partner - me_range)) * BEAMS + pair_place
 
     def send_tile(j, i, peer):
         column = row_of(j) * SIDE_AZ + i
@@ -330,34 +336,40 @@
         @pl.when((peer != me_range) | (column != me_az))
         def _():
             remote(
-                tiles(ready, (j * SIDE_AZ + i) * GROUP + peer, 1), tiles(arrived, whole_beam(j), 1),
+                tiles(ready, (j * SIDE_AZ + i) * GROUP + peer, 1), tiles(arrived, beam_of(j), 1),
                 hist_send, hist_recv, range=peer, az=column,
             ).start()
 
-    def send_tiles(j, half):
-        away = half != me_range // HALF
-        high, low = me_range // 4 - 2 * (me_range // HALF), lax.rem(me_range // 2, 2)
-        for turn in range(4):
-            t1, t0 = jnp.where(away, turn // 2, 1 - turn // 2), jnp.where(away, turn % 2, 1 - turn % 2)
-            plane = 2 * (high + t1 - 2 * high * t1) + low + t0 - 2 * low * t0
-
-            def column(k, carry):
-                for c in (1, 0):
-                    send_tile(j, lax.rem(x + k, SIDE_AZ), half * HALF + 2 * plane + c)
-                return carry
-
-            lax.fori_loop(0, SIDE_AZ, column, 0)
+    def send_tiles(j):
+        own_block = j < 2
+
+        def column(k, carry):
+            i = lax.rem(x + k, SIDE_AZ)
+            for step in (3, -3, 2, -2, 1, -1, 0):
+                plane = lax.rem(z + step + 8, 8)
+                close = jnp.where(core == 0, step in (-1, 0, 1, 2), step in (-2, -1, 0, 1))
+                to_early = plane < 4
+                wanted = (own_block & (close | (early & to_early))) | (
+                    jnp.logical_not(own_block) & close & (early | jnp.logical_not(to_early))
+                )
+
+                @pl.when(wanted)
+                def _():
+                    for c in (1, 0):
+                        send_tile(j, i, 2 * plane + c)
+
+            return carry
+
+        lax.fori_loop(0, SIDE_AZ, column, 0)
 
     def work(j, carry):
         @pl.when(j == 2)
         def _():
-            remote(fifteen, fifteen, pulse_send, pulse_recv.at[1], az=me_az).wait_recv()
-
-        e_left, e_right = phases(j)
-        specs = [spectrum(e_left, e_right, i) for i in range(SIDE_AZ)]
-        source = jnp.where(j == 2, 1, 0)
-        pulse = [gathered[source, :, part].reshape(SIDE, SIDE) for part in range(2)]
-        mine = iota((1, SIDE), 1) == whole_beam(j)
+            wait_pulses(1)
+
+        specs = [spec[j * SIDE_AZ + i] for i in range(SIDE_AZ)]
+        pulse = [gathered[j // 2, :, part].reshape(SIDE, SIDE) for part in range(2)]
+        mine = iota((1, SIDE), 1) == beam_of(j)
         ambient = jnp.sum(jnp.where(mine, ambient_ref[...], 0.0), axis=1, keepdims=True)
         hist = group_histogram(
             specs, [pulse] * SIDE_AZ, [ambient] * SIDE_AZ, left_tab[...], right_tab[...],
@@ -365,59 +377,45 @@
         )
         ready[tiles_of(j * SIDE_AZ * GROUP, SIDE_AZ * GROUP), :] = hist
 
-        @pl.when(early & (j == 0))
+        @pl.when(j == 0)
+        def _():
+            pl.semaphore_wait(near_sem, HALF - 1)
+
+        send_tiles(j)
+
+        @pl.when(j == 0)
         def _():
             extra_copy.wait_recv()
-            lax.fori_loop(1, GROUP, share_extra, 0)
-            gathered[1, me_az] = extra[beam_of(2)]
-
-        @pl.when(j == 0)
+            share(extra, 1)
+            gathered[1, me_az] = extra[pair_place]
+
+        @pl.when(j == 1)
         def _():
-            pl.when(early)(pass_on)
-            pl.semaphore_wait(near_sem, HALF - 1)
-
-        @pl.when(early | (j == 0))
-        def _():
-            send_tiles(j, 0)
-
-        @pl.when(j == 0)
-        def _():
-            send_tiles(0, 1)
-
-        @pl.when((j == jnp.where(early, 2, 1)))
-        def _():
-            send_tiles(1, 1)
+            lax.fori_loop(2, 4, prepare, 0)
 
         return carry
 
-    lax.fori_loop(0, jnp.where(early, 3, 2), work, 0)
-
-    def keep(j):
-        arrived[tiles_of(whole_beam(j), 1), :] = ready[
-            tiles_of((j * SIDE_AZ + x) * GROUP + me_range, 1), :
-        ]
+    lax.fori_loop(0, 4, work, 0)
+    kept = [
+        pltpu.make_async_copy(
+            tiles(ready, (j * SIDE_AZ + x) * GROUP + me_range, 1), tiles(arrived, beam_of(j), 1),
+            keep_sem.at[j // 2],
+        )
+        for j in (0, 2)
+    ]
+    for copy in kept:
+        copy.start()
 
     def settled(ref, send, recv, count):
         some = tiles(ref, 0, count)
         return remote(some, some, send, recv, az=me_az)
 
-    keep(0)
-
-    @pl.when(early)
-    def _():
-        keep(2)
-        settled(arrived, hist_send, hist_recv, GROUP * BEAMS - 2).wait_recv()
-
-    @pl.when(late)
-    def _():
-        settled(arrived, hist_send, hist_recv, GROUP * BEAMS - 1).wait_recv()
-
-    for g in range(GROUP):
-        for s in range(8):
-            out_ref[0, g * 8 : (g + 1) * 8, s * SIDE : (s + 1) * SIDE] = arrived[
-                pl.ds(g * 64 + s, 8, stride=8), :
-            ]
-    remote(fifteen, fifteen, pulse_send, pulse_recv.at[0], az=me_az).wait_send()
+    settled(arrived, hist_send, hist_recv, GROUP * BEAMS - 2).wait_recv()
+    for copy in kept:
+        copy.wait()
+    for which in range(2):
+        remote(fifteen, fifteen, pulse_send, pulse_recv.at[which], az=me_az).wait_send()
+    extra_copy.wait_send()
     seven = echoes.at[pl.ds(0, HALF - 1)]
     remote(seven, seven, echo_send, echo_recv, az=me_az).wait_send()
 
@@ -425,28 +423,50 @@
     def _():
         remote(some_echoes, some_echoes, echo_send, echo_recv, az=me_az).wait_send()
 
-    tiles_all, tiles_half = SIDE_AZ * GROUP, SIDE_AZ * HALF
-
-    @pl.when(early)
-    def _():
-        remote(fifteen, fifteen, pulse_send, pulse_recv.at[1], az=me_az).wait_send()
-        settled(ready, hist_send, hist_recv, 2 * tiles_all + tiles_half - 2).wait_send()
-
-    @pl.when(late)
-    def _():
-        extra_copy.wait_send()
-        settled(ready, hist_send, hist_recv, tiles_all + tiles_half - 1).wait_send()
+    settled(ready, hist_send, hist_recv, 14).wait_send()
+    aside = jnp.abs(lax.rem(z, 4) - 1 - core)
+
+    def sent(i, carry):
+        settled(ready, hist_send, hist_recv, 16).wait_send()
+        return carry
+
+    lax.fori_loop(0, 7 + jnp.where(early, aside, -aside), sent, 0)
+
+
+def spread(arrived, out_ref, tiles, rows, in_sem, out_sem):
+    step = GROUP * BEAMS // PIECES
+    fetches = [
+        pltpu.make_async_copy(
+            arrived.at[pl.ds(k * step * 8, step * 8)], tiles.at[pl.ds(k * step * 8, step * 8)], in_sem.at[k]
+        )
+        for k in range(PIECES)
+    ]
+    for fetch in fetches:
+        fetch.start()
+    stores = []
+    for k, fetch in enumerate(fetches):
+        fetch.wait()
+        for g in range(k * step // 8, (k + 1) * step // 8):
+            for s in range(8):
+                rows[0, g * 8 : (g + 1) * 8, s * SIDE : (s + 1) * SIDE] = tiles[
+                    pl.ds(g * 64 + s, 8, stride=8), :
+                ]
+        some = pl.ds(k * step, step)
+        stores.append(pltpu.make_async_copy(rows.at[:, some], out_ref.at[:, some], out_sem.at[k]))
+        stores[-1].start()
+    for store in stores:
+        store.wait()
 
 
 def per_device(lag, frac, amp, offset, count, ambient, pulse):
     lag, frac, amp = [jnp.swapaxes(v, 1, 2) for v in (lag, frac, amp)]
     hbm = pl.BlockSpec(memory_space=pltpu.HBM)
     dma = pltpu.SemaphoreType.DMA
-    return pl.pallas_call(
+    arrived = pl.pallas_call(
         kernel,
-        out_shape=jax.ShapeDtypeStruct((1, GROUP * BEAMS, TIME_SLOTS // GROUP), F32),
+        out_shape=jax.ShapeDtypeStruct((GROUP * BEAMS * 8, SIDE), F32),
         in_specs=[hbm] * 6,
-        out_specs=pl.BlockSpec(memory_space=pltpu.VMEM),
+        out_specs=hbm,
         scratch_shapes=[
             pltpu.VMEM((1, SLOTS, SIDE), jnp.int32),
             pltpu.VMEM((1, SLOTS, SIDE), F32),
@@ -458,20 +478,32 @@
             pltpu.VMEM((GROUP, SLOTS, SIDE), F32),
             pltpu.VMEM((2, GROUP, 2, 8, SIDE), F32),
             pltpu.VMEM((BEAMS, 2, 8, SIDE), F32),
+            pltpu.VMEM((2 * BEAMS, 2 * SIDE, 2 * SIDE), F32),
             pltpu.VMEM((2 * SIDE, 6 * SIDE), BF16),
             pltpu.VMEM((6 * SIDE, 2 * SIDE), BF16),
             pltpu.VMEM((2, SIDE, SIDE), F32),
             pltpu.VMEM((2 * SIDE, 2 * SIDE), BF16),
             pltpu.VMEM((SIDE, 2 * SIDE), BF16),
-            pltpu.VMEM((3 * SIDE_AZ * SIDE, SIDE), F32),
-            pltpu.VMEM((GROUP * BEAMS * 8, SIDE), F32),
-            dma((6,)), dma, dma, dma, dma, dma, dma((2,)), dma, dma,
+            pltpu.VMEM((4 * SIDE_AZ * SIDE, SIDE), F32),
+            dma((6,)), dma((2,)), dma, dma, dma, dma, dma, dma((2,)), dma, dma,
             pltpu.SemaphoreType.REGULAR, pltpu.SemaphoreType.REGULAR,
         ],
         compiler_params=pltpu.CompilerParams(
-            collective_id=0, has_side_effects=True, vmem_limit_bytes=40 * 1024 * 1024
+            collective_id=0, has_side_effects=True, vmem_limit_bytes=VMEM_LIMIT
         ),
     )(lag, frac, amp, (offset * 16 + count).reshape(1, 1), ambient.reshape(1, SIDE), pulse)
+    return pl.pallas_call(
+        spread,
+        out_shape=jax.ShapeDtypeStruct((1, GROUP * BEAMS, TIME_SLOTS // GROUP), F32),
+        in_specs=[hbm],
+        out_specs=hbm,
+        scratch_shapes=[
+            pltpu.VMEM((GROUP * BEAMS * 8, SIDE), F32),
+            pltpu.VMEM((1, GROUP * BEAMS, TIME_SLOTS // GROUP), F32),
+            dma((PIECES,)), dma((PIECES,)),
+        ],
+        compiler_params=pltpu.CompilerParams(vmem_limit_bytes=VMEM_LIMIT),
+    )(arrived)
 
 
 def solution(mesh):

time: 36.5 us -> 33.9 us (0.929)
  local copies, waits for them, and re-layouts: 2.32 us -> 0 us
    unnamed x11 -> x0, local copies, waits for them, and re-layouts: 2.32 us -> none
    pallas_call x1 -> x2, Pallas kernels: 32.6 us -> 32.5 us  [the longest x1 30.6 us: per_device(): pl.pallas_call(kernel, out_shape=jax.ShapeDtypeStruct((GROUP * BEAMS * 8,...]
where the time goes in v6:
time: 33.9 us; the launch traced here: 33.8 us
  Pallas kernels  32.5 us (96%)
  between operations  1.31 us (4%)
    pallas_call x1, Pallas kernels, per_device(): pl.pallas_call(kernel, out_shape=jax.ShapeDtypeStruct((GROUP * BEAMS * 8,...  30.6 us
    pallas_call x1, Pallas kernels, per_device(): pl.pallas_call(spread, out_shape=jax.ShapeDtypeStruct((1, GROUP * BEAMS,...  1.84 us

profile of v6, /device:TPU:1, one launch (start us, length us, event | category | flops | bytes accessed | tf_op | source)
XLA Modules:
  0.0 33.8 jit_solution(11515644029232025902)
XLA Ops:
  1.3 30.6 %shard_map.73.arrived = f32[1024,128]{1,0:T(8,128)} custom-call(s32[1,8,128]{2,1,0:T(8,128)} %bitcast.5, f32[1,8,128]{2,1,0:T(8,128)} %bitcast.6, f32[1,8,128]{2,1,0:T(8,128)} %bitcast.7, s32[1,1]{1,0:T(1,128)} %bitcast.3.packed_hbm, f32[1,128]{1,0:T(1,128)} %bitcast.8, f32[8,2,1024]{2,1,0:T(2,128)} %pulse_hbm.1), custom_call_target="tpu_custom_call" | custom-call | tf_op jit(solution)/shard_map/pallas_call | solution.py:465
  31.9 1.8 %shard_map.74 = f32[1,128,1024]{2,1,0:T(8,128)} custom-call(f32[1024,128]{1,0:T(8,128)} %shard_map.73.arrived), custom_call_target="tpu_custom_call" | custom-call | tf_op jit(solution)/shard_map/pallas_call | solution.py:495

commit v7 on v4

--- a/solution.py
+++ b/solution.py
@@ -13,7 +13,9 @@
 SLOTS = 8
 GROUP = 16
 HALF = 8
-EARLY_ORDER = (1, 0, 7, 6, 3, 2, 5, 4)
+PIECES = 4
+VMEM_LIMIT = 56 * 1024 * 1024
+EARLY_ORDER = (1, 0, 3, 2, 7, 6, 5, 4)
 LATE_ORDER = (8, 9, 14, 15, 10, 11, 12, 13)
 SIDE_AZ = 4
 MESH = pl.DeviceIdType.MESH
@@ -156,11 +158,11 @@
 
 def kernel(
     lag_hbm, frac_hbm, amp_hbm, packed_hbm, ambient_hbm, pulse_hbm,
-    out_ref,
+    arrived,
     lag_ref, frac_ref, amp_ref, packed_ref, ambient_ref, pulse_ref,
     own, gathered, extra, left_tab, right_tab, twist_tab, inner_tab, outer_tab,
-    ready, arrived,
-    in_sem, extra_send, extra_recv, pulse_send, pulse_recv, hist_send, hist_recv, go_sem, near_sem,
+    ready,
+    in_sem, keep_sem, extra_send, extra_recv, pulse_send, pulse_recv, hist_send, hist_recv, go_sem, near_sem,
 ):
     me_range, me_az = lax.axis_index("range"), lax.axis_index("az")
     y, x = me_az // SIDE_AZ, lax.rem(me_az, SIDE_AZ)
@@ -315,13 +317,9 @@
             ).start()
 
     def send_tiles(j, order):
-        def column(k, carry):
-            i = lax.rem(x + k, SIDE_AZ)
-            for peer in order:
-                send_tile(j, i, peer)
-            return carry
-
-        lax.fori_loop(0, SIDE_AZ, column, 0)
+        for peer in order:
+            for k in range(SIDE_AZ):
+                send_tile(j, lax.rem(x + k, SIDE_AZ), peer)
 
     def work(j, carry):
         @pl.when(j > 0)
@@ -344,19 +342,22 @@
         def _():
             pl.semaphore_wait(near_sem, SIDE_AZ - 1)
 
-        @pl.when(early | (j == 0))
-        def _():
-            send_tiles(j, EARLY_ORDER)
-
         @pl.when(early & (j == 0))
         def _():
             extra_copy.wait_recv()
             lax.fori_loop(1, GROUP, share_extra, 0)
             gathered[2, me_az, :2] = extra[x]
 
-        @pl.when(j == 1)
+        @pl.when(early | (j == 0))
+        def _():
+            send_tiles(j, EARLY_ORDER)
+
+        @pl.when(j == 0)
         def _():
             send_tiles(0, LATE_ORDER)
+
+        @pl.when((j == jnp.where(early, 2, 1)))
+        def _():
             send_tiles(1, LATE_ORDER)
 
         return carry
@@ -364,29 +365,31 @@
     lax.fori_loop(0, jnp.where(early, 3, 2), work, 0)
 
     def keep(j):
-        arrived[tiles_of(beam_of(j), 1), :] = ready[tiles_of((j * SIDE_AZ + x) * GROUP + me_range, 1), :]
+        return pltpu.make_async_copy(
+            tiles(ready, (j * SIDE_AZ + x) * GROUP + me_range, 1), tiles(arrived, beam_of(j), 1),
+            keep_sem.at[j],
+        )
 
     def settled(ref, send, recv, count):
         some = tiles(ref, 0, count)
         return remote(some, some, send, recv, az=me_az)
 
-    keep(0)
-    keep(1)
+    keep(0).start()
+    keep(1).start()
 
     @pl.when(early)
     def _():
-        keep(2)
+        keep(2).start()
         settled(arrived, hist_send, hist_recv, GROUP * BEAMS - 3).wait_recv()
+        keep(2).wait()
 
     @pl.when(late)
     def _():
         settled(arrived, hist_send, hist_recv, GROUP * BEAMS - 2).wait_recv()
 
-    for g in range(GROUP):
-        for s in range(8):
-            out_ref[0, g * 8 : (g + 1) * 8, s * SIDE : (s + 1) * SIDE] = arrived[
-                pl.ds(g * 64 + s, 8, stride=8), :
-            ]
+    keep(0).wait()
+    keep(1).wait()
+
     some = gathered.at[0, pl.ds(0, GROUP - 1)]
     remote(some, some, pulse_send, pulse_recv.at[0], az=me_az).wait_send()
     some = gathered.at[1, pl.ds(0, GROUP - 1), parts]
@@ -404,15 +407,40 @@
         settled(ready, hist_send, hist_recv, tiles_all + tiles_half).wait_send()
 
 
+def spread(arrived, out_ref, tiles, rows, in_sem, out_sem):
+    step = GROUP * BEAMS // PIECES
+    fetches = [
+        pltpu.make_async_copy(
+            arrived.at[pl.ds(k * step * 8, step * 8)], tiles.at[pl.ds(k * step * 8, step * 8)], in_sem.at[k]
+        )
+        for k in range(PIECES)
+    ]
+    for fetch in fetches:
+        fetch.start()
+    stores = []
+    for k, fetch in enumerate(fetches):
+        fetch.wait()
+        for g in range(k * step // 8, (k + 1) * step // 8):
+            for s in range(8):
+                rows[0, g * 8 : (g + 1) * 8, s * SIDE : (s + 1) * SIDE] = tiles[
+                    pl.ds(g * 64 + s, 8, stride=8), :
+                ]
+        some = pl.ds(k * step, step)
+        stores.append(pltpu.make_async_copy(rows.at[:, some], out_ref.at[:, some], out_sem.at[k]))
+        stores[-1].start()
+    for store in stores:
+        store.wait()
+
+
 def per_device(lag, frac, amp, offset, count, ambient, pulse):
     lag, frac, amp = [jnp.swapaxes(v, 1, 2) for v in (lag, frac, amp)]
     hbm = pl.BlockSpec(memory_space=pltpu.HBM)
     dma = pltpu.SemaphoreType.DMA
-    return pl.pallas_call(
+    arrived = pl.pallas_call(
         kernel,
-        out_shape=jax.ShapeDtypeStruct((1, GROUP * BEAMS, TIME_SLOTS // GROUP), F32),
+        out_shape=jax.ShapeDtypeStruct((GROUP * BEAMS * 8, SIDE), F32),
         in_specs=[hbm] * 6,
-        out_specs=pl.BlockSpec(memory_space=pltpu.VMEM),
+        out_specs=hbm,
         scratch_shapes=[
             pltpu.VMEM((1, SLOTS, SIDE), jnp.int32),
             pltpu.VMEM((1, SLOTS, SIDE), F32),
@@ -429,14 +457,25 @@
             pltpu.VMEM((2 * SIDE, 2 * SIDE), BF16),
             pltpu.VMEM((SIDE, 2 * SIDE), BF16),
             pltpu.VMEM((3 * SIDE_AZ * SIDE, SIDE), F32),
-            pltpu.VMEM((GROUP * BEAMS * 8, SIDE), F32),
-            dma((6,)), dma, dma, dma, dma((3,)), dma, dma,
+            dma((6,)), dma((3,)), dma, dma, dma, dma((3,)), dma, dma,
             pltpu.SemaphoreType.REGULAR, pltpu.SemaphoreType.REGULAR,
         ],
         compiler_params=pltpu.CompilerParams(
-            collective_id=0, has_side_effects=True, vmem_limit_bytes=40 * 1024 * 1024
+            collective_id=0, has_side_effects=True, vmem_limit_bytes=VMEM_LIMIT
         ),
     )(lag, frac, amp, (offset * 16 + count).reshape(1, 1), ambient.reshape(1, SIDE), pulse)
+    return pl.pallas_call(
+        spread,
+        out_shape=jax.ShapeDtypeStruct((1, GROUP * BEAMS, TIME_SLOTS // GROUP), F32),
+        in_specs=[hbm],
+        out_specs=hbm,
+        scratch_shapes=[
+            pltpu.VMEM((GROUP * BEAMS * 8, SIDE), F32),
+            pltpu.VMEM((1, GROUP * BEAMS, TIME_SLOTS // GROUP), F32),
+            dma((PIECES,)), dma((PIECES,)),
+        ],
+        compiler_params=pltpu.CompilerParams(vmem_limit_bytes=VMEM_LIMIT),
+    )(arrived)
 
 
 def solution(mesh):

time: 35.9 us -> 33.4 us (0.930)
  local copies, waits for them, and re-layouts: 2.32 us -> 0 us
    unnamed x11 -> x0, local copies, waits for them, and re-layouts: 2.32 us -> none
    pallas_call x1 -> x2, Pallas kernels: 32.1 us -> 31.9 us  [the longest x1 30.1 us: per_device(): pl.pallas_call(kernel, out_shape=jax.ShapeDtypeStruct((GROUP * BEAMS * 8,...]
where the time goes in v7:
time: 33.4 us; the launch traced here: 33.3 us
  Pallas kernels  31.9 us (96%)
  between operations  1.31 us (4%)
    pallas_call x1, Pallas kernels, per_device(): pl.pallas_call(kernel, out_shape=jax.ShapeDtypeStruct((GROUP * BEAMS * 8,...  30.1 us
    pallas_call x1, Pallas kernels, per_device(): pl.pallas_call(spread, out_shape=jax.ShapeDtypeStruct((1, GROUP * BEAMS,...  1.84 us

profile of v7, /device:TPU:1, one launch (start us, length us, event | category | flops | bytes accessed | tf_op | source)
XLA Modules:
  0.0 33.3 jit_solution(1951504443568831185)
XLA Ops:
  1.3 30.1 %shard_map.73.arrived = f32[1024,128]{1,0:T(8,128)} custom-call(s32[1,8,128]{2,1,0:T(8,128)} %bitcast.5, f32[1,8,128]{2,1,0:T(8,128)} %bitcast.6, f32[1,8,128]{2,1,0:T(8,128)} %bitcast.7, s32[1,1]{1,0:T(1,128)} %bitcast.3.packed_hbm, f32[1,128]{1,0:T(1,128)} %bitcast.8, f32[8,2,1024]{2,1,0:T(2,128)} %pulse_hbm.1), custom_call_target="tpu_custom_call" | custom-call | tf_op jit(solution)/shard_map/pallas_call | solution.py:439
  31.4 1.8 %shard_map.74 = f32[1,128,1024]{2,1,0:T(8,128)} custom-call(f32[1024,128]{1,0:T(8,128)} %shard_map.73.arrived), custom_call_target="tpu_custom_call" | custom-call | tf_op jit(solution)/shard_map/pallas_call | solution.py:467

commit v8 on v7

--- a/solution.py
+++ b/solution.py
@@ -13,6 +13,7 @@
 SLOTS = 8
 GROUP = 16
 HALF = 8
+FAR_FIRST = (10, 6, 9, 11, 14, 2, 8, 5, 7, 13, 15, 1, 3, 4, 12)
 PIECES = 4
 VMEM_LIMIT = 56 * 1024 * 1024
 EARLY_ORDER = (1, 0, 3, 2, 7, 6, 5, 4)
@@ -160,7 +161,7 @@
     lag_hbm, frac_hbm, amp_hbm, packed_hbm, ambient_hbm, pulse_hbm,
     arrived,
     lag_ref, frac_ref, amp_ref, packed_ref, ambient_ref, pulse_ref,
-    own, gathered, extra, left_tab, right_tab, twist_tab, inner_tab, outer_tab,
+    own, gathered, extra, spec, left_tab, right_tab, twist_tab, inner_tab, outer_tab,
     ready,
     in_sem, keep_sem, extra_send, extra_recv, pulse_send, pulse_recv, hist_send, hist_recv, go_sem, near_sem,
 ):
@@ -255,8 +256,10 @@
         remote(mine, gathered.at[2, me_az, parts], pulse_send, pulse_recv.at[2], az=peer).start()
         return carry
 
-    lax.fori_loop(1, GROUP, share, 0)
-    lax.fori_loop(1, GROUP, share_next, 0)
+    for k in FAR_FIRST:
+        share(k, 0)
+    for k in FAR_FIRST:
+        share_next(k, 0)
 
     @pl.when(me_range == chief)
     def _():
@@ -322,13 +325,16 @@
                 send_tile(j, lax.rem(x + k, SIDE_AZ), peer)
 
     def work(j, carry):
+        e_left, e_right = phases(j)
+        for i in range(SIDE_AZ):
+            spec[i] = spectrum(e_left, e_right, i)
+
         @pl.when(j > 0)
         def _():
             some = gathered.at[1, pl.ds(0, GROUP - 1), parts]
             remote(some, some, pulse_send, pulse_recv.at[j], az=me_az).wait_recv()
 
-        e_left, e_right = phases(j)
-        specs = [spectrum(e_left, e_right, i) for i in range(SIDE_AZ)]
+        specs = [spec[i] for i in range(SIDE_AZ)]
         pulse = [gathered[j, :, part].reshape(SIDE, SIDE) for part in range(2)]
         mine = iota((1, SIDE), 1) == beam_of(j)
         ambient = jnp.sum(jnp.where(mine, ambient_ref[...], 0.0), axis=1, keepdims=True)
@@ -345,7 +351,8 @@
         @pl.when(early & (j == 0))
         def _():
             extra_copy.wait_recv()
-            lax.fori_loop(1, GROUP, share_extra, 0)
+            for k in FAR_FIRST:
+                share_extra(k, 0)
             gathered[2, me_az, :2] = extra[x]
 
         @pl.when(early | (j == 0))
@@ -451,6 +458,7 @@
             pltpu.VMEM((2, SIDE_AZ, 3, 8, SIDE), F32),
             pltpu.VMEM((3, GROUP, 3, 8, SIDE), F32),
             pltpu.VMEM((SIDE_AZ, 2, 8, SIDE), F32),
+            pltpu.VMEM((SIDE_AZ, 2 * SIDE, 2 * SIDE), F32),
             pltpu.VMEM((2 * SIDE, 6 * SIDE), BF16),
             pltpu.VMEM((6 * SIDE, 2 * SIDE), BF16),
             pltpu.VMEM((2, SIDE, SIDE), F32),

time: 33.4 us -> 32.9 us (0.985)
  Pallas kernels: 31.9 us -> 31.5 us
    pallas_call x1, Pallas kernels: 30.1 us -> 29.6 us  [per_device(): pl.pallas_call(kernel, out_shape=jax.ShapeDtypeStruct((GROUP * BEAMS * 8,...]
where the time goes in v8:
time: 32.9 us; the launch traced here: 32.8 us
  Pallas kernels  31.5 us (96%)
  between operations  1.31 us (4%)
    pallas_call x1, Pallas kernels, per_device(): pl.pallas_call(kernel, out_shape=jax.ShapeDtypeStruct((GROUP * BEAMS * 8,...  29.6 us
    pallas_call x1, Pallas kernels, per_device(): pl.pallas_call(spread, out_shape=jax.ShapeDtypeStruct((1, GROUP * BEAMS,...  1.84 us

profile of v8, /device:TPU:1, one launch (start us, length us, event | category | flops | bytes accessed | tf_op | source)
XLA Modules:
  0.0 32.8 jit_solution(13174174037943420097)
XLA Ops:
  1.3 29.6 %shard_map.73.arrived = f32[1024,128]{1,0:T(8,128)} custom-call(s32[1,8,128]{2,1,0:T(8,128)} %bitcast.5, f32[1,8,128]{2,1,0:T(8,128)} %bitcast.6, f32[1,8,128]{2,1,0:T(8,128)} %bitcast.7, s32[1,1]{1,0:T(1,128)} %bitcast.3.packed_hbm, f32[1,128]{1,0:T(1,128)} %bitcast.8, f32[8,2,1024]{2,1,0:T(2,128)} %pulse_hbm.1), custom_call_target="tpu_custom_call" | custom-call | tf_op jit(solution)/shard_map/pallas_call | solution.py:446
  30.9 1.8 %shard_map.74 = f32[1,128,1024]{2,1,0:T(8,128)} custom-call(f32[1024,128]{1,0:T(8,128)} %shard_map.73.arrived), custom_call_target="tpu_custom_call" | custom-call | tf_op jit(solution)/shard_map/pallas_call | solution.py:475

commit v9 on v8

--- a/solution.py
+++ b/solution.py
@@ -231,6 +231,15 @@
         barrier,
         GROUP - 1 + jnp.where(early, 0, 1) + jnp.where(me_range == chief, GROUP - 1, 0),
     )
+
+    @pl.when(me_range == chief)
+    def _():
+        def tell(k, carry):
+            pl.semaphore_signal(go_sem, inc=1, device_id={"range": k}, device_id_type=MESH)
+            return carry
+
+        lax.fori_loop(0, GROUP - 1, tell, 0)
+
     parts = pl.ds(0, 2)
     extra_copy = remote(own.at[1, :, parts], extra, extra_send, extra_recv, range=partner)
 
@@ -260,14 +269,6 @@
         share(k, 0)
     for k in FAR_FIRST:
         share_next(k, 0)
-
-    @pl.when(me_range == chief)
-    def _():
-        def tell(k, carry):
-            pl.semaphore_signal(go_sem, inc=1, device_id={"range": k}, device_id_type=MESH)
-            return carry
-
-        lax.fori_loop(0, GROUP - 1, tell, 0)
 
     gathered[0, me_az] = own[0, x]
     gathered[1, me_az] = own[1, x]

time: 32.9 us -> 33.1 us (level)
  no operation moved by 1% of the time
where the time goes in v9:
time: 33.1 us; the launch traced here: 33 us
  Pallas kernels  31.7 us (96%)
  between operations  1.31 us (4%)
    pallas_call x1, Pallas kernels, per_device(): pl.pallas_call(kernel, out_shape=jax.ShapeDtypeStruct((GROUP * BEAMS * 8,...  29.8 us
    pallas_call x1, Pallas kernels, per_device(): pl.pallas_call(spread, out_shape=jax.ShapeDtypeStruct((1, GROUP * BEAMS,...  1.84 us

profile of v9, /device:TPU:1, one launch (start us, length us, event | category | flops | bytes accessed | tf_op | source)
XLA Modules:
  0.0 33.0 jit_solution(9779410756689190600)
XLA Ops:
  1.3 29.8 %shard_map.73.arrived = f32[1024,128]{1,0:T(8,128)} custom-call(s32[1,8,128]{2,1,0:T(8,128)} %bitcast.5, f32[1,8,128]{2,1,0:T(8,128)} %bitcast.6, f32[1,8,128]{2,1,0:T(8,128)} %bitcast.7, s32[1,1]{1,0:T(1,128)} %bitcast.3.packed_hbm, f32[1,128]{1,0:T(1,128)} %bitcast.8, f32[8,2,1024]{2,1,0:T(2,128)} %pulse_hbm.1), custom_call_target="tpu_custom_call" | custom-call | tf_op jit(solution)/shard_map/pallas_call | solution.py:447
  31.1 1.8 %shard_map.74 = f32[1,128,1024]{2,1,0:T(8,128)} custom-call(f32[1024,128]{1,0:T(8,128)} %shard_map.73.arrived), custom_call_target="tpu_custom_call" | custom-call | tf_op jit(solution)/shard_map/pallas_call | solution.py:476

commit v10 on v8

--- a/solution.py
+++ b/solution.py
@@ -234,9 +234,6 @@
     parts = pl.ds(0, 2)
     extra_copy = remote(own.at[1, :, parts], extra, extra_send, extra_recv, range=partner)
 
-    @pl.when(late)
-    def _():
-        extra_copy.start()
 
     def share(k, carry):
         peer = lax.rem(me_az + k, GROUP)
@@ -258,6 +255,11 @@
 
     for k in FAR_FIRST:
         share(k, 0)
+
+    @pl.when(late)
+    def _():
+        extra_copy.start()
+
     for k in FAR_FIRST:
         share_next(k, 0)
 

time: 32.9 us -> 32.9 us (level)
  no operation moved by 1% of the time
where the time goes in v10:
time: 32.9 us; the launch traced here: 32.8 us
  Pallas kernels  31.5 us (96%)
  between operations  1.31 us (4%)
    pallas_call x1, Pallas kernels, per_device(): pl.pallas_call(kernel, out_shape=jax.ShapeDtypeStruct((GROUP * BEAMS * 8,...  29.6 us
    pallas_call x1, Pallas kernels, per_device(): pl.pallas_call(spread, out_shape=jax.ShapeDtypeStruct((1, GROUP * BEAMS,...  1.84 us

profile of v10, /device:TPU:1, one launch (start us, length us, event | category | flops | bytes accessed | tf_op | source)
XLA Modules:
  0.0 32.8 jit_solution(11896762460458826498)
XLA Ops:
  1.3 29.6 %shard_map.73.arrived = f32[1024,128]{1,0:T(8,128)} custom-call(s32[1,8,128]{2,1,0:T(8,128)} %bitcast.5, f32[1,8,128]{2,1,0:T(8,128)} %bitcast.6, f32[1,8,128]{2,1,0:T(8,128)} %bitcast.7, s32[1,1]{1,0:T(1,128)} %bitcast.3.packed_hbm, f32[1,128]{1,0:T(1,128)} %bitcast.8, f32[8,2,1024]{2,1,0:T(2,128)} %pulse_hbm.1), custom_call_target="tpu_custom_call" | custom-call | tf_op jit(solution)/shard_map/pallas_call | solution.py:448
  30.9 1.8 %shard_map.74 = f32[1,128,1024]{2,1,0:T(8,128)} custom-call(f32[1024,128]{1,0:T(8,128)} %shard_map.73.arrived), custom_call_target="tpu_custom_call" | custom-call | tf_op jit(solution)/shard_map/pallas_call | solution.py:477
